TPU v7x, 32 devices: a whole 2x2x4 slice. The times are simulated.
32 devices in a mesh: comp: 2 (over x), face: 16 (over z, y, core).
Axes of the slice: x: 2, y: 2, z: 4, core: 2. Of those that a mesh axis runs over, the one named last changes fastest.
Arguments:
- state: bfloat16 [2, 16, 4096], P('comp', None, 'face'), may hold values from -6 to 6
- cotangent: bfloat16 [2, 16, 4096], P('comp', None, 'face'), may hold values from -6 to 6
- land_sea: int32 [4096], P('face'), may hold values 0 or 1
- turn_table: int32 [16, 4], replicated, may hold values from 0 to 3
- first_kernel: bfloat16 [2, 216, 256], P('comp'), may hold values from -0.625 to 0.625
- mid_kernel: bfloat16 [2, 2304, 256], P('comp'), may hold values from -0.1875 to 0.1875
- out_kernel: bfloat16 [2, 2304, 16], P('comp'), may hold values from -0.1875 to 0.1875
- first_gates: int32 [2, 216, 64], P('comp'), may hold values from 0 to 5
- mid_gates: int32 [2, 2304, 64], P('comp'), may hold values from 0 to 5
- out_gates: int32 [2, 2304, 4], P('comp'), may hold values from 0 to 5
Outputs:
- upcoming_climate_estimate: bfloat16 [2, 16, 4096], P('comp', None, 'face')
- condition_adjoint_grid: float32 [2, 16, 4096], P('comp', None, 'face')
- opening_filter_adjoint: float32 [2, 216, 256], P('comp')
- central_filter_adjoint: float32 [2, 589824], P('comp', 'face')
- closing_filter_adjoint: float32 [2, 36864], P('comp', 'face')
Inputs may be any that keep to these rules, and one draw needn't show every extreme that they name: `mid_gates`: a gate value picks one of the six ways of keeping 2 of 4 consecutive output channels. `first_gates`: a gate value picks one of the six ways of keeping 2 of 4 consecutive output channels. `out_gates`: a gate value picks one of the six ways of keeping 2 of 4 consecutive output channels.
All inputs are finite; a program needn't handle non-finite values. No bound on the sum of `land_sea` on one device may be relied on, other than what follows from the above.
Results may differ from a plain program's by a relative error of at most 0.0052.
Values may be sent and summed in bfloat16 or wider, within the bound.
A program may use at most 64 MiB of HBM per device.

v0:
```python
import jax
import jax.numpy as jnp
from jax import lax
from jax.sharding import PartitionSpec as P

FIELDS = 16
COUPLED = 8
ROW_TILES = 4
TS = 16


EDGE_MAP = (
    ((0, False), (2, True), (1, True), (3, False)),
    ((1, False), (3, True), (0, True), (2, False)),
    ((2, False), (1, False), (3, True), (0, True)),
    ((3, False), (0, False), (2, True), (1, True)),
)


def shifted(value, axis, steps):
    count = lax.axis_size(axis)
    pairs = [(source, (source + steps) % count) for source in range(count)]
    return lax.ppermute(value, axis, pairs)


def partner_2(block, axis, distance):
    count = lax.axis_size(axis)
    route = []
    for low in range(count):
        high = low | 1 << distance
        if high != low and high < count:
            route += [(low, high), (high, low)]
    return lax.ppermute(block, axis, route)


def gate_pair(gates):
    low = (gates >= 3).astype(jnp.int32) + (gates >= 5).astype(jnp.int32)
    high = jnp.where(gates == 0, 1, jnp.where((gates == 1) | (gates == 3), 2, 3)).astype(jnp.int32)
    return (low, high)


def gate_keep(gates):
    low, high = gate_pair(gates)
    lanes = jnp.arange(4, dtype=jnp.int32)
    keep = (low[..., None] == lanes) | (high[..., None] == lanes)
    return keep.reshape(gates.shape[0], gates.shape[1] * 4)


def raw_edges(square):
    return (square[:, :, -1], square[:, :, 0], square[:, -1, :], square[:, 0, :])


def take_edge(square, turn, side):
    edges = raw_edges(square)
    picked = jnp.zeros_like(edges[0])
    for turns in range(4):
        slot, flip = EDGE_MAP[side][turns]
        candidate = edges[slot][:, ::-1] if flip else edges[slot]
        picked = jnp.where(turn == turns, candidate, picked)
    return picked


def add_strip(slots, strip, turn, side):
    slots = list(slots)
    for turns in range(4):
        slot, flip = EDGE_MAP[side][turns]
        candidate = strip[:, ::-1] if flip else strip
        slots[slot] = slots[slot] + jnp.where(turn == turns, candidate, 0.0)
    return slots


def turn_for(turn_table, offset, side):
    here = lax.axis_index("face")
    count = lax.axis_size("face")
    return turn_table[jnp.remainder(here + offset, count), side]


def with_halo(square, turn_table):
    west = shifted(take_edge(square, turn_for(turn_table, 1, 0), 0), "face", 1)
    east = shifted(take_edge(square, turn_for(turn_table, -1, 1), 1), "face", -1)
    south = shifted(take_edge(square, turn_for(turn_table, ROW_TILES, 2), 2), "face", ROW_TILES)
    north = shifted(take_edge(square, turn_for(turn_table, -ROW_TILES, 3), 3), "face", -ROW_TILES)
    padded = jnp.pad(square, ((0, 0), (1, 1), (1, 1)))
    padded = padded.at[:, 1:-1, 0].set(west)
    padded = padded.at[:, 1:-1, -1].set(east)
    padded = padded.at[:, 0, 1:-1].set(south)
    padded = padded.at[:, -1, 1:-1].set(north)
    return padded


def without_halo(dpad, turn_table):
    breadth_count = dpad.shape[1] - 2
    inner = dpad[:, 1:-1, 1:-1]
    slots = [jnp.zeros((dpad.shape[0], breadth_count), jnp.float32) for index in range(4)]
    from_east = shifted(dpad[:, 1:-1, 0], "face", -1)
    slots = add_strip(slots, from_east, turn_for(turn_table, 1, 0), 0)
    from_west = shifted(dpad[:, 1:-1, -1], "face", 1)
    slots = add_strip(slots, from_west, turn_for(turn_table, -1, 1), 1)
    from_north = shifted(dpad[:, 0, 1:-1], "face", -ROW_TILES)
    slots = add_strip(slots, from_north, turn_for(turn_table, ROW_TILES, 2), 2)
    from_south = shifted(dpad[:, -1, 1:-1], "face", ROW_TILES)
    slots = add_strip(slots, from_south, turn_for(turn_table, -ROW_TILES, 3), 3)
    inner = inner.at[:, :, -1].add(slots[0])
    inner = inner.at[:, :, 0].add(slots[1])
    inner = inner.at[:, -1, :].add(slots[2])
    inner = inner.at[:, 0, :].add(slots[3])
    return inner.reshape(inner.shape[0], breadth_count * breadth_count)


def unfold(padded, breadth_count):
    feature_depth = padded.shape[0]
    return jnp.concatenate(
        [
            padded[
                :,
                vertical_place : vertical_place + breadth_count,
                horizontal_place : horizontal_place + breadth_count,
            ].reshape(feature_depth, breadth_count * breadth_count)
            for vertical_place in range(3)
            for horizontal_place in range(3)
        ],
        0,
    )


def fold(columns, feature_depth, breadth_count):
    prognosis_outcome = jnp.zeros(
        (feature_depth, breadth_count + 2, breadth_count + 2), jnp.float32
    )
    index = 0
    for vertical_place in range(3):
        for horizontal_place in range(3):
            square_piece = columns[index * feature_depth : (index + 1) * feature_depth].reshape(
                feature_depth, breadth_count, breadth_count
            )
            prognosis_outcome = prognosis_outcome.at[
                :,
                vertical_place : vertical_place + breadth_count,
                horizontal_place : horizontal_place + breadth_count,
            ].add(square_piece)
            index = index + 1
    return prognosis_outcome


def convolve_stencil(kernel, columns):
    return lax.dot_general(
        kernel, columns, (((0,), (0,)), ((), ())), preferred_element_type=jnp.float32
    )


def kernel_term(columns, grad):
    return lax.dot_general(
        columns, grad, (((1,), (1,)), ((), ())), preferred_element_type=jnp.float32
    )


def slope(values):
    sig = jax.nn.sigmoid(values)
    return sig * (1.0 + values * (1.0 - sig))


def body(
    state,
    cotangent,
    land_sea,
    turn_table,
    first_kernel,
    mid_kernel,
    out_kernel,
    first_gates,
    mid_gates,
    out_gates,
):
    breadth_count = TS
    comp = lax.axis_index("comp")
    zero_half = jnp.zeros((), jnp.bfloat16)
    zero_float = jnp.zeros((), jnp.float32)
    local_region_quantity = state[0]
    partner = partner_2(local_region_quantity[:COUPLED], "comp", 0)
    inputs = jnp.concatenate([local_region_quantity, partner], 0)
    sea = land_sea.astype(jnp.float32)
    scaling_ratio = jnp.where(comp == 1, sea, jnp.ones_like(sea))
    opening_keep = gate_keep(first_gates[0])
    central_keep = gate_keep(mid_gates[0])
    closing_keep = gate_keep(out_gates[0])
    kernel_first = jnp.where(opening_keep, first_kernel[0], zero_half)
    kernel_mid = jnp.where(central_keep, mid_kernel[0], zero_half)
    stencil_produced = jnp.where(closing_keep, out_kernel[0], zero_half)
    in_channels = inputs.shape[0]
    hidden = kernel_mid.shape[1]
    columns_zero = unfold(
        with_halo(inputs.reshape(in_channels, breadth_count, breadth_count), turn_table),
        breadth_count,
    )
    act_one = convolve_stencil(kernel_first, columns_zero)
    hid_one = jax.nn.silu(act_one).astype(jnp.bfloat16)
    columns_one = unfold(
        with_halo(hid_one.reshape(hidden, breadth_count, breadth_count), turn_table), breadth_count
    )
    act_two = convolve_stencil(kernel_mid, columns_one)
    hid_two = jax.nn.silu(act_two).astype(jnp.bfloat16)
    vertical_bands_two = unfold(
        with_halo(hid_two.reshape(hidden, breadth_count, breadth_count), turn_table), breadth_count
    )
    prognosis_outcome = convolve_stencil(stencil_produced, vertical_bands_two)
    upcoming_climate_estimate = (
        local_region_quantity.astype(jnp.float32) + scaling_ratio * prognosis_outcome
    ).astype(jnp.bfloat16)
    cot_float = cotangent[0].astype(jnp.float32)
    grad_three = (scaling_ratio * cot_float).astype(jnp.bfloat16)
    out_local = jnp.where(closing_keep, kernel_term(vertical_bands_two, grad_three), zero_float)
    output_extent = lax.psum_scatter(out_local.reshape(-1), "face", scatter_dimension=0, tiled=True)
    back_two = fold(
        jnp.dot(stencil_produced, grad_three, preferred_element_type=jnp.float32),
        hidden,
        breadth_count,
    )
    grad_hid_two = without_halo(back_two, turn_table)
    grad_two = (grad_hid_two * slope(act_two)).astype(jnp.bfloat16)
    mid_local = jnp.where(central_keep, kernel_term(columns_one, grad_two), zero_float)
    middle_extent = lax.psum_scatter(mid_local.reshape(-1), "face", scatter_dimension=0, tiled=True)
    back_one = fold(
        jnp.dot(kernel_mid, grad_two, preferred_element_type=jnp.float32), hidden, breadth_count
    )
    grad_hid_one = without_halo(back_one, turn_table)
    grad_one = (grad_hid_one * slope(act_one)).astype(jnp.bfloat16)
    first_local = jnp.where(opening_keep, kernel_term(columns_zero, grad_one), zero_float)
    back_zero = fold(
        jnp.dot(kernel_first, grad_one, preferred_element_type=jnp.float32),
        in_channels,
        breadth_count,
    )
    grad_inputs = without_halo(back_zero, turn_table)
    returned = partner_2(grad_inputs[FIELDS:], "comp", 0)
    own_domain_adjoint = cot_float + grad_inputs[:FIELDS]
    own_domain_adjoint = own_domain_adjoint.at[:COUPLED].add(returned)
    leading_gate_total = lax.psum(first_local, "face")
    return (
        upcoming_climate_estimate[None],
        own_domain_adjoint[None],
        leading_gate_total[None],
        middle_extent[None],
        output_extent[None],
    )


def solution(mesh):
    in_specs = (
        P("comp", None, "face"),
        P("comp", None, "face"),
        P("face"),
        P(),
        P("comp", None, None),
        P("comp", None, None),
        P("comp", None, None),
        P("comp", None, None),
        P("comp", None, None),
        P("comp", None, None),
    )
    out_specs = (
        P("comp", None, "face"),
        P("comp", None, "face"),
        P("comp", None, None),
        P("comp", "face"),
        P("comp", "face"),
    )
    return jax.shard_map(body, mesh=mesh, in_specs=in_specs, out_specs=out_specs, check_vma=False)
```

profile of v0, /device:TPU:0, one launch (start us, length us, event | category | flops | bytes accessed | tf_op | source)
XLA Modules:
  0.0 280.5 jit_solution(12646320055255744950)
XLA Ops:
  7.2 1.3 slice_bitcast_fusion.10
  8.5 2.9 %collective-permute-start = (bf16[8,256]{1,0:T(8,128)(2,1)}, bf16[8,256]{1,0:T(8,128)(2,1)}, u32[]{:S(2)}, u32[]{:S(2)}) collective-permute-start(bf16[8,256]{1,0:T(8,128)(2,1)} %slice_bitcast_fusion.10), channel_id=1, source_target_pairs={{0,16},{16,0},{1,17},{17,1},{2,18},{18,2},{3,19},{19,3},{4,20},{20... | collective-permute-start | bytes 12296 | tf_op jit(solution)/shard_map/ppermute | solution.py:33
  13.8 1.4 fusion.12
  17.0 1.4 copy_add_fusion.1
  18.4 1.6 scatter-add.135
  20.0 2.0 add_select_fusion.1
  22.0 1.6 scatter-add.136
  28.0 3.6 %collective-permute-start.15 = (f32[256,16]{0,1:T(8,128)}, f32[256,16]{0,1:T(8,128)}, u32[]{:S(2)}, u32[]{:S(2)}) collective-permute-start(f32[256,16]{0,1:T(8,128)} %bitcast.261), channel_id=1, source_target_pairs={{0,12},{1,13},{2,14},{3,15},{4,0},{5,1},{6,2},{7,3},{8,4},{9,5},{1... | collective-permute-start | bytes 49160 | tf_op jit(solution)/shard_map/ppermute | solution.py:23
  35.9 1.9 eq.457
  37.8 2.0 copy.620
  39.8 1.8 eq.466
  41.7 3.4 %eq.467 = s32[2304,256]{0,1:T(8,128)} reshape(s32[2304,64,4]{0,2,1:T(4,128)} %eq.466) | data formatting | bytes 4718592 | tf_op jit(solution)/shard_map/eq | solution.py:45
  45.1 3.1 %copy.621 = s32[2304,256]{1,0:T(8,128)} copy(s32[2304,256]{0,1:T(8,128)} %eq.467) | data formatting | bytes 4718592 | tf_op jit(solution)/shard_map/eq | solution.py:45
  48.3 2.1 compare_or_fusion
  51.2 1.5 constant_dynamic-slice_fusion.2
  64.3 4.5 %collective-permute-start.2 = (bf16[24,16]{0,1:T(8,128)(2,1)S(1)}, bf16[24,16]{0,1:T(8,128)(2,1)S(1)}, u32[]{:S(2)}, u32[]{:S(2)}) collective-permute-start(bf16[24,16]{0,1:T(8,128)(2,1)S(1)} %get-tuple-element.729), channel_id=1, source_target_pairs={{0,15},{1,0},{2,1},{3,2},{4,3},{5,4},{6,5},{7,6},{8,7},{9,8},{10,9... | collective-permute-start | bytes 2312 | tf_op jit(solution)/shard_map/ppermute | solution.py:23
  68.7 3.8 %collective-permute-start.4 = (bf16[24,16]{0,1:T(8,128)(2,1)S(1)}, bf16[24,16]{0,1:T(8,128)(2,1)S(1)}, u32[]{:S(2)}, u32[]{:S(2)}) collective-permute-start(bf16[24,16]{0,1:T(8,128)(2,1)S(1)} %get-tuple-element.726), channel_id=1, source_target_pairs={{0,12},{1,13},{2,14},{3,15},{4,0},{5,1},{6,2},{7,3},{8,4},{9,5},{1... | collective-permute-start | bytes 2312 | tf_op jit(solution)/shard_map/ppermute | solution.py:23
  74.9 4.0 %scatter.41 = bf16[24,18,18]{2,1,0:T(8,128)(2,1)S(1)} dynamic-update-slice(bf16[24,18,18]{2,1,0:T(8,128)(2,1)S(1)} %scatter.40, bf16[24,16,1]{2,1,0:T(8,128)(2,1)S(1)} %copy.629, s32[]{:T(128)} %constant.1326.clone.1, s32[]{:T(128)} %constant.1322.clone.1, s32[]{:T(128)} %constant.1337.clone.1) | dynamic-update-slice | bytes 1540 | tf_op jit(solution)/shard_map/scatter | solution.py:85
  78.9 5.0 %scatter.44 = bf16[24,18,18]{2,1,0:T(8,128)(2,1)S(1)} dynamic-update-slice(bf16[24,18,18]{2,1,0:T(8,128)(2,1)S(1)} %scatter.41, bf16[24,1,16]{2,1,0:T(2,128)(2,1)S(1)} %copy.630, s32[]{:T(128)} %constant.1326.clone.1, s32[]{:T(128)} %bitcast.30, s32[]{:T(128)} %bitcast.31) | dynamic-update-slice | bytes 1540 | tf_op jit(solution)/shard_map/scatter | solution.py:86
  83.9 3.7 %scatter.45 = bf16[24,18,18]{2,1,0:T(8,128)(2,1)S(1)} dynamic-update-slice(bf16[24,18,18]{2,1,0:T(8,128)(2,1)S(1)} %scatter.44, bf16[24,1,16]{2,1,0:T(2,128)(2,1)S(1)} %copy.631, s32[]{:T(128)} %constant.1326.clone.1, s32[]{:T(128)} %constant.1337.clone.1, s32[]{:T(128)} %constant.1322.clone.1) | dynamic-update-slice | bytes 1540 | tf_op jit(solution)/shard_map/scatter | solution.py:87
  91.3 3.8 %collective-permute-start.8 = (bf16[256,16]{0,1:T(8,128)(2,1)S(1)}, bf16[256,16]{0,1:T(8,128)(2,1)S(1)}, u32[]{:S(2)}, u32[]{:S(2)}) collective-permute-start(bf16[256,16]{0,1:T(8,128)(2,1)S(1)} %get-tuple-element.634), channel_id=1, source_target_pairs={{0,12},{1,13},{2,14},{3,15},{4,0},{5,1},{6,2},{7,3},{8,4},{9,5},{1... | collective-permute-start | bytes 24584 | tf_op jit(solution)/shard_map/ppermute | solution.py:23
  98.1 4.5 %collective-permute-start.13 = (f32[256,16]{0,1:T(8,128)}, f32[256,16]{0,1:T(8,128)S(1)}, u32[]{:S(2)}, u32[]{:S(2)}) collective-permute-start(f32[256,16]{0,1:T(8,128)} %get-tuple-element.660), channel_id=1, source_target_pairs={{0,15},{1,0},{2,1},{3,2},{4,3},{5,4},{6,5},{7,6},{8,7},{9,8},{10,9... | collective-permute-start | bytes 49160 | tf_op jit(solution)/shard_map/ppermute | solution.py:23
  102.6 1.4 scatter.50
  105.8 2.6 fusion.10
  110.2 2.1 copy_add_fusion
  112.3 2.4 scatter-add.156
  114.8 3.0 %add_select_fusion = f32[256,16,16]{0,1,2:T(8,128)S(1)} fusion(f32[256,16,16]{0,2,1:T(8,128)} %bitcast.285, f32[256,18,18]{0,1,2:T(8,128)S(1)} %scatter-add.156, s32[]{:T(128)} %bitcast.74, s32[]{:T(128)} %bitcast.75, pred[]{:T(512)} %and_reduce_fusion), kind=kLoop, calls=%fused_computation.17 | loop fusion | flops 131072 | bytes 786441 | tf_op jit(solution)/shard_map/select.79
  117.7 1.6 scatter-add.159
  119.3 1.9 slice_add_fusion.5
  121.2 1.2 scatter-add.160
  122.4 1.8 slice_add_fusion.4
  124.2 1.2 scatter-add.161
  126.3 1.2 scatter-add.164
  129.6 4.0 %collective-permute-start.10 = (bf16[256,16]{0,1:T(8,128)(2,1)S(1)}, bf16[256,16]{0,1:T(8,128)(2,1)S(1)}, u32[]{:S(2)}, u32[]{:S(2)}) collective-permute-start(bf16[256,16]{0,1:T(8,128)(2,1)S(1)} %get-tuple-element.698), channel_id=1, source_target_pairs={{0,15},{1,0},{2,1},{3,2},{4,3},{5,4},{6,5},{7,6},{8,7},{9,8},{10,9... | collective-permute-start | bytes 24584 | tf_op jit(solution)/shard_map/ppermute | solution.py:23
  133.5 3.8 %collective-permute-start.12 = (bf16[256,16]{0,1:T(8,128)(2,1)S(1)}, bf16[256,16]{0,1:T(8,128)(2,1)S(1)}, u32[]{:S(2)}, u32[]{:S(2)}) collective-permute-start(bf16[256,16]{0,1:T(8,128)(2,1)S(1)} %get-tuple-element.632), channel_id=1, source_target_pairs={{0,12},{1,13},{2,14},{3,15},{4,0},{5,1},{6,2},{7,3},{8,4},{9,5},{1... | collective-permute-start | bytes 24584 | tf_op jit(solution)/shard_map/ppermute | solution.py:23
  138.0 2.6 copy.690
  140.6 2.0 collective-permute-start.20
  142.9 4.5 %collective-permute-start.17 = (f32[256,16]{0,1:T(8,128)S(1)}, f32[256,16]{0,1:T(8,128)S(1)}, u32[]{:S(2)}, u32[]{:S(2)}) collective-permute-start(f32[256,16]{0,1:T(8,128)S(1)} %get-tuple-element.656), channel_id=1, source_target_pairs={{0,15},{1,0},{2,1},{3,2},{4,3},{5,4},{6,5},{7,6},{8,7},{9,8},{10,9... | collective-permute-start | bytes 49160 | tf_op jit(solution)/shard_map/ppermute | solution.py:23
  147.4 1.4 scatter.56
  154.4 1.3 dynamic-slice_add_fusion
  155.9 1.5 scatter-add.179
  157.4 1.9 add_select_fusion.2
  159.3 1.5 scatter-add.180
  164.4 3.6 %collective-permute-start.23 = (f32[24,16]{0,1:T(8,128)S(1)}, f32[24,16]{0,1:T(8,128)S(1)}, u32[]{:S(2)}, u32[]{:S(2)}) collective-permute-start(f32[24,16]{0,1:T(8,128)S(1)} %bitcast.341), channel_id=1, source_target_pairs={{0,12},{1,13},{2,14},{3,15},{4,0},{5,1},{6,2},{7,3},{8,4},{9,5},{1... | collective-permute-start | bytes 4616 | tf_op jit(solution)/shard_map/ppermute | solution.py:23
  171.2 3.0 %collective-permute-done.25 = f32[8,256]{1,0:T(8,128)S(1)} collective-permute-done((f32[8,256]{1,0:T(8,128)S(1)}, f32[8,256]{1,0:T(8,128)S(1)}, u32[]{:S(2)}, u32[]{:S(2)}) %collective-permute-start.25) | collective-permute-done | bytes 8224 | tf_op jit(solution)/shard_map/ppermute | solution.py:33
  174.2 94.9 %all-reduce.11.cloned.1.call-done = (f32[1,216,256]{2,1,0:T(8,128)}, f32[589824]{0:T(1024)}, f32[36864]{0:T(1024)}) async-done(((f32[1,216,256]{2,1,0:T(8,128)}, f32[589824]{0:T(1024)}, f32[36864]{0:T(1024)}), (f32[1,216,256]{2,1,0:T(8,128)}, f32[589824]{0:T(1024)}, f32[36864]{0:T(1024)})) %all-reduce.11.cloned.1.call-update) | async-done | bytes 2727952 | tf_op jit(solution)/shard_map/psum | solution.py:237
  270.5 1.6 dynamic-slice.412
  272.0 1.6 copy.810
  (341 shorter events, 42.9 us)
Async XLA Ops:
  7.2 261.9 %all-reduce.11.cloned.1.call-start = ((), (), s32[]{:S(2)}) async-start(), calls=%async_computation | async-start | bytes 5455872 | tf_op jit(solution)/shard_map/psum | solution.py:237
  8.5 54.1 %collective-permute-start = (bf16[8,256]{1,0:T(8,128)(2,1)}, bf16[8,256]{1,0:T(8,128)(2,1)}, u32[]{:S(2)}, u32[]{:S(2)}) collective-permute-start(bf16[8,256]{1,0:T(8,128)(2,1)} %slice_bitcast_fusion.10), channel_id=1, source_target_pairs={{0,16},{16,0},{1,17},{17,1},{2,18},{18,2},{3,19},{19,3},{4,20},{20... | collective-permute-start | bytes 12296 | tf_op jit(solution)/shard_map/ppermute | solution.py:33
  13.8 1.4 copy-start.22
  25.7 5.9 %copy-start.18 = (bf16[1,16,256]{2,1,0:T(8,128)(2,1)S(1)}, bf16[1,16,256]{2,1,0:T(8,128)(2,1)}, u32[]{:S(2)}) copy-start(bf16[1,16,256]{2,1,0:T(8,128)(2,1)} %param.114) | copy-start | bytes 24580
  26.3 6.9 %copy-start.16 = (s32[1,216,64]{1,2,0:T(8,128)S(1)}, s32[1,216,64]{1,2,0:T(8,128)}, u32[]{:S(2)}) copy-start(s32[1,216,64]{1,2,0:T(8,128)} %param.121) | copy-start | bytes 165892
  28.0 76.5 %collective-permute-start.15 = (f32[256,16]{0,1:T(8,128)}, f32[256,16]{0,1:T(8,128)}, u32[]{:S(2)}, u32[]{:S(2)}) collective-permute-start(f32[256,16]{0,1:T(8,128)} %bitcast.261), channel_id=1, source_target_pairs={{0,12},{1,13},{2,14},{3,15},{4,0},{5,1},{6,2},{7,3},{8,4},{9,5},{1... | collective-permute-start | bytes 49160 | tf_op jit(solution)/shard_map/ppermute | solution.py:23
  33.3 2.0 copy-start.4
  45.1 3.2 %copy-start.2 = (s32[216,256]{1,0:T(8,128)S(1)}, s32[216,256]{1,0:T(8,128)}, u32[]{:S(2)}) copy-start(s32[216,256]{1,0:T(8,128)} %copy.622) | copy-start | bytes 663556
  45.1 3.2 %copy-start.3 = (s32[216,256]{1,0:T(8,128)S(1)}, s32[216,256]{1,0:T(8,128)}, u32[]{:S(2)}) copy-start(s32[216,256]{1,0:T(8,128)} %copy.623) | copy-start | bytes 663556
  48.3 2.1 copy-start.5
  48.3 2.1 copy-start.6
  64.1 9.2 %collective-permute-start.1 = (bf16[24,16]{0,1:T(8,128)(2,1)S(1)}, bf16[24,16]{0,1:T(8,128)(2,1)S(1)}, u32[]{:S(2)}, u32[]{:S(2)}) collective-permute-start(bf16[24,16]{0,1:T(8,128)(2,1)S(1)} %get-tuple-element.727), channel_id=1, source_target_pairs={{0,1},{1,2},{2,3},{3,4},{4,5},{5,6},{6,7},{7,8},{8,9},{9,10},{10,1... | collective-permute-start | bytes 2312 | tf_op jit(solution)/shard_map/ppermute | solution.py:23
  64.3 9.3 %collective-permute-start.2 = (bf16[24,16]{0,1:T(8,128)(2,1)S(1)}, bf16[24,16]{0,1:T(8,128)(2,1)S(1)}, u32[]{:S(2)}, u32[]{:S(2)}) collective-permute-start(bf16[24,16]{0,1:T(8,128)(2,1)S(1)} %get-tuple-element.729), channel_id=1, source_target_pairs={{0,15},{1,0},{2,1},{3,2},{4,3},{5,4},{6,5},{7,6},{8,7},{9,8},{10,9... | collective-permute-start | bytes 2312 | tf_op jit(solution)/shard_map/ppermute | solution.py:23
  68.7 5.4 %collective-permute-start.3 = (bf16[24,16]{0,1:T(8,128)(2,1)S(1)}, bf16[24,16]{0,1:T(8,128)(2,1)S(1)}, u32[]{:S(2)}, u32[]{:S(2)}) collective-permute-start(bf16[24,16]{0,1:T(8,128)(2,1)S(1)} %get-tuple-element.728), channel_id=1, source_target_pairs={{0,4},{1,5},{2,6},{3,7},{4,8},{5,9},{6,10},{7,11},{8,12},{9,13},{1... | collective-permute-start | bytes 2312 | tf_op jit(solution)/shard_map/ppermute | solution.py:23
  68.7 5.5 %collective-permute-start.4 = (bf16[24,16]{0,1:T(8,128)(2,1)S(1)}, bf16[24,16]{0,1:T(8,128)(2,1)S(1)}, u32[]{:S(2)}, u32[]{:S(2)}) collective-permute-start(bf16[24,16]{0,1:T(8,128)(2,1)S(1)} %get-tuple-element.726), channel_id=1, source_target_pairs={{0,12},{1,13},{2,14},{3,15},{4,0},{5,1},{6,2},{7,3},{8,4},{9,5},{1... | collective-permute-start | bytes 2312 | tf_op jit(solution)/shard_map/ppermute | solution.py:23
  87.6 1.7 copy-start.14
  88.9 6.2 %copy-start.13 = (bf16[1,16,256]{2,1,0:T(8,128)(2,1)S(1)}, bf16[1,16,256]{2,1,0:T(8,128)(2,1)}, u32[]{:S(2)}) copy-start(bf16[1,16,256]{2,1,0:T(8,128)(2,1)} %param.115) | copy-start | bytes 24580
  89.3 6.5 %copy-start.11 = (bf16[216,256]{1,0:T(8,128)(2,1)}, bf16[216,256]{1,0:T(8,128)(2,1)S(1)}, u32[]{:S(2)}) copy-start(bf16[216,256]{1,0:T(8,128)(2,1)S(1)} %constant_dynamic-update-slice_fusion.2) | copy-start | bytes 331780
  89.3 6.5 %copy-start.17 = (f32[256,1,16]{0,1,2:T(1,128)S(1)}, f32[256,1,16]{0,1,2:T(1,128)}, u32[]{:S(2)}) copy-start(f32[256,1,16]{0,1,2:T(1,128)} %get-tuple-element.663) | copy-start | bytes 49156
  89.3 6.5 %copy-start.25 = (u32[32]{0:T(128)S(1)}, u32[32]{0:T(128)}, u32[]{:S(2)}) copy-start(u32[32]{0:T(128)} %constant.1366) | copy-start | bytes 388
  90.7 7.1 %collective-permute-start.6 = (bf16[256,16]{0,1:T(8,128)(2,1)S(1)}, bf16[256,16]{0,1:T(8,128)(2,1)S(1)}, u32[]{:S(2)}, u32[]{:S(2)}) collective-permute-start(bf16[256,16]{0,1:T(8,128)(2,1)S(1)} %get-tuple-element.700), channel_id=1, source_target_pairs={{0,15},{1,0},{2,1},{3,2},{4,3},{5,4},{6,5},{7,6},{8,7},{9,8},{10,9... | collective-permute-start | bytes 24584 | tf_op jit(solution)/shard_map/ppermute | solution.py:23
  91.3 6.6 %collective-permute-start.5 = (bf16[256,16]{0,1:T(8,128)(2,1)S(1)}, bf16[256,16]{0,1:T(8,128)(2,1)S(1)}, u32[]{:S(2)}, u32[]{:S(2)}) collective-permute-start(bf16[256,16]{0,1:T(8,128)(2,1)S(1)} %select_select_fusion.7), channel_id=1, source_target_pairs={{0,1},{1,2},{2,3},{3,4},{4,5},{5,6},{6,7},{7,8},{8,9},{9,10},{10,1... | collective-permute-start | bytes 24584 | tf_op jit(solution)/shard_map/ppermute | solution.py:23
  91.3 6.8 %collective-permute-start.7 = (bf16[256,16]{0,1:T(8,128)(2,1)S(1)}, bf16[256,16]{0,1:T(8,128)(2,1)S(1)}, u32[]{:S(2)}, u32[]{:S(2)}) collective-permute-start(bf16[256,16]{0,1:T(8,128)(2,1)S(1)} %get-tuple-element.699), channel_id=1, source_target_pairs={{0,4},{1,5},{2,6},{3,7},{4,8},{5,9},{6,10},{7,11},{8,12},{9,13},{1... | collective-permute-start | bytes 24584 | tf_op jit(solution)/shard_map/ppermute | solution.py:23
  91.3 12.8 %collective-permute-start.8 = (bf16[256,16]{0,1:T(8,128)(2,1)S(1)}, bf16[256,16]{0,1:T(8,128)(2,1)S(1)}, u32[]{:S(2)}, u32[]{:S(2)}) collective-permute-start(bf16[256,16]{0,1:T(8,128)(2,1)S(1)} %get-tuple-element.634), channel_id=1, source_target_pairs={{0,12},{1,13},{2,14},{3,15},{4,0},{5,1},{6,2},{7,3},{8,4},{9,5},{1... | collective-permute-start | bytes 24584 | tf_op jit(solution)/shard_map/ppermute | solution.py:23
  97.7 7.6 %collective-permute-start.16 = (f32[256,16]{0,1:T(8,128)S(1)}, f32[256,16]{0,1:T(8,128)S(1)}, u32[]{:S(2)}, u32[]{:S(2)}) collective-permute-start(f32[256,16]{0,1:T(8,128)S(1)} %bitcast.329), channel_id=1, source_target_pairs={{0,4},{1,5},{2,6},{3,7},{4,8},{5,9},{6,10},{7,11},{8,12},{9,13},{1... | collective-permute-start | bytes 49160 | tf_op jit(solution)/shard_map/ppermute | solution.py:23
  97.8 7.4 %collective-permute-start.14 = (f32[256,16]{0,1:T(8,128)}, f32[256,16]{0,1:T(8,128)S(1)}, u32[]{:S(2)}, u32[]{:S(2)}) collective-permute-start(f32[256,16]{0,1:T(8,128)} %get-tuple-element.661), channel_id=1, source_target_pairs={{0,1},{1,2},{2,3},{3,4},{4,5},{5,6},{6,7},{7,8},{8,9},{9,10},{10,1... | collective-permute-start | bytes 49160 | tf_op jit(solution)/shard_map/ppermute | solution.py:23
  98.1 7.3 %collective-permute-start.13 = (f32[256,16]{0,1:T(8,128)}, f32[256,16]{0,1:T(8,128)S(1)}, u32[]{:S(2)}, u32[]{:S(2)}) collective-permute-start(f32[256,16]{0,1:T(8,128)} %get-tuple-element.660), channel_id=1, source_target_pairs={{0,15},{1,0},{2,1},{3,2},{4,3},{5,4},{6,5},{7,6},{8,7},{9,8},{10,9... | collective-permute-start | bytes 49160 | tf_op jit(solution)/shard_map/ppermute | solution.py:23
  105.8 2.6 copy-start
  119.3 6.1 %copy-start.1 = (f32[256,256]{0,1:T(8,128)S(1)}, f32[256,256]{0,1:T(8,128)}, u32[]{:S(2)}) copy-start(f32[256,256]{0,1:T(8,128)} %get-tuple-element.639) | copy-start | bytes 786436
  129.6 11.0 %collective-permute-start.10 = (bf16[256,16]{0,1:T(8,128)(2,1)S(1)}, bf16[256,16]{0,1:T(8,128)(2,1)S(1)}, u32[]{:S(2)}, u32[]{:S(2)}) collective-permute-start(bf16[256,16]{0,1:T(8,128)(2,1)S(1)} %get-tuple-element.698), channel_id=1, source_target_pairs={{0,15},{1,0},{2,1},{3,2},{4,3},{5,4},{6,5},{7,6},{8,7},{9,8},{10,9... | collective-permute-start | bytes 24584 | tf_op jit(solution)/shard_map/ppermute | solution.py:23
  133.5 9.1 %collective-permute-start.9 = (bf16[256,16]{0,1:T(8,128)(2,1)S(1)}, bf16[256,16]{0,1:T(8,128)(2,1)S(1)}, u32[]{:S(2)}, u32[]{:S(2)}) collective-permute-start(bf16[256,16]{0,1:T(8,128)(2,1)S(1)} %select_select_fusion.3), channel_id=1, source_target_pairs={{0,1},{1,2},{2,3},{3,4},{4,5},{5,6},{6,7},{7,8},{8,9},{9,10},{10,1... | collective-permute-start | bytes 24584 | tf_op jit(solution)/shard_map/ppermute | solution.py:23
  133.5 9.4 %collective-permute-start.11 = (bf16[256,16]{0,1:T(8,128)(2,1)S(1)}, bf16[256,16]{0,1:T(8,128)(2,1)S(1)}, u32[]{:S(2)}, u32[]{:S(2)}) collective-permute-start(bf16[256,16]{0,1:T(8,128)(2,1)S(1)} %get-tuple-element.697), channel_id=1, source_target_pairs={{0,4},{1,5},{2,6},{3,7},{4,8},{5,9},{6,10},{7,11},{8,12},{9,13},{1... | collective-permute-start | bytes 24584 | tf_op jit(solution)/shard_map/ppermute | solution.py:23
  133.5 15.3 %collective-permute-start.12 = (bf16[256,16]{0,1:T(8,128)(2,1)S(1)}, bf16[256,16]{0,1:T(8,128)(2,1)S(1)}, u32[]{:S(2)}, u32[]{:S(2)}) collective-permute-start(bf16[256,16]{0,1:T(8,128)(2,1)S(1)} %get-tuple-element.632), channel_id=1, source_target_pairs={{0,12},{1,13},{2,14},{3,15},{4,0},{5,1},{6,2},{7,3},{8,4},{9,5},{1... | collective-permute-start | bytes 24584 | tf_op jit(solution)/shard_map/ppermute | solution.py:23
  140.6 12.1 %collective-permute-start.19 = (f32[256,16]{0,1:T(8,128)S(1)}, f32[256,16]{0,1:T(8,128)S(1)}, u32[]{:S(2)}, u32[]{:S(2)}) collective-permute-start(f32[256,16]{0,1:T(8,128)S(1)} %bitcast.331), channel_id=1, source_target_pairs={{0,12},{1,13},{2,14},{3,15},{4,0},{5,1},{6,2},{7,3},{8,4},{9,5},{1... | collective-permute-start | bytes 49160 | tf_op jit(solution)/shard_map/ppermute | solution.py:23
  140.6 12.2 %collective-permute-start.20 = (f32[256,16]{0,1:T(8,128)S(1)}, f32[256,16]{0,1:T(8,128)S(1)}, u32[]{:S(2)}, u32[]{:S(2)}) collective-permute-start(f32[256,16]{0,1:T(8,128)S(1)} %bitcast.330), channel_id=1, source_target_pairs={{0,4},{1,5},{2,6},{3,7},{4,8},{5,9},{6,10},{7,11},{8,12},{9,13},{1... | collective-permute-start | bytes 49160 | tf_op jit(solution)/shard_map/ppermute | solution.py:23
  142.6 10.1 %collective-permute-start.18 = (f32[256,16]{0,1:T(8,128)S(1)}, f32[256,16]{0,1:T(8,128)S(1)}, u32[]{:S(2)}, u32[]{:S(2)}) collective-permute-start(f32[256,16]{0,1:T(8,128)S(1)} %get-tuple-element.657), channel_id=1, source_target_pairs={{0,1},{1,2},{2,3},{3,4},{4,5},{5,6},{6,7},{7,8},{8,9},{9,10},{10,1... | collective-permute-start | bytes 49160 | tf_op jit(solution)/shard_map/ppermute | solution.py:23
  142.9 10.0 %collective-permute-start.17 = (f32[256,16]{0,1:T(8,128)S(1)}, f32[256,16]{0,1:T(8,128)S(1)}, u32[]{:S(2)}, u32[]{:S(2)}) collective-permute-start(f32[256,16]{0,1:T(8,128)S(1)} %get-tuple-element.656), channel_id=1, source_target_pairs={{0,15},{1,0},{2,1},{3,2},{4,3},{5,4},{6,5},{7,6},{8,7},{9,8},{10,9... | collective-permute-start | bytes 49160 | tf_op jit(solution)/shard_map/ppermute | solution.py:23
  149.3 0.9 copy-start.9
  151.6 1.8 copy-start.10
  152.6 0.9 copy-start.15
  162.9 5.1 %copy-start.12 = (bf16[216,256]{1,0:T(8,128)(2,1)S(1)}, bf16[216,256]{1,0:T(8,128)(2,1)}, u32[]{:S(2)}) copy-start(bf16[216,256]{1,0:T(8,128)(2,1)} %copy-done.11) | copy-start | bytes 331780
  163.9 6.2 %collective-permute-start.21 = (f32[24,16]{0,1:T(8,128)S(1)}, f32[24,16]{0,1:T(8,128)S(1)}, u32[]{:S(2)}, u32[]{:S(2)}) collective-permute-start(f32[24,16]{0,1:T(8,128)S(1)} %get-tuple-element.666), channel_id=1, source_target_pairs={{0,15},{1,0},{2,1},{3,2},{4,3},{5,4},{6,5},{7,6},{8,7},{9,8},{10,9... | collective-permute-start | bytes 4616 | tf_op jit(solution)/shard_map/ppermute | solution.py:23
  164.2 5.8 %collective-permute-start.24 = (f32[24,16]{0,1:T(8,128)S(1)}, f32[24,16]{0,1:T(8,128)S(1)}, u32[]{:S(2)}, u32[]{:S(2)}) collective-permute-start(f32[24,16]{0,1:T(8,128)S(1)} %bitcast.340), channel_id=1, source_target_pairs={{0,4},{1,5},{2,6},{3,7},{4,8},{5,9},{6,10},{7,11},{8,12},{9,13},{1... | collective-permute-start | bytes 4616 | tf_op jit(solution)/shard_map/ppermute | solution.py:23
  164.2 5.8 %collective-permute-start.22 = (f32[24,16]{0,1:T(8,128)S(1)}, f32[24,16]{0,1:T(8,128)S(1)}, u32[]{:S(2)}, u32[]{:S(2)}) collective-permute-start(f32[24,16]{0,1:T(8,128)S(1)} %get-tuple-element.667), channel_id=1, source_target_pairs={{0,1},{1,2},{2,3},{3,4},{4,5},{5,6},{6,7},{7,8},{8,9},{9,10},{10,1... | collective-permute-start | bytes 4616 | tf_op jit(solution)/shard_map/ppermute | solution.py:23
  164.4 5.6 %collective-permute-start.23 = (f32[24,16]{0,1:T(8,128)S(1)}, f32[24,16]{0,1:T(8,128)S(1)}, u32[]{:S(2)}, u32[]{:S(2)}) collective-permute-start(f32[24,16]{0,1:T(8,128)S(1)} %bitcast.341), channel_id=1, source_target_pairs={{0,12},{1,13},{2,14},{3,15},{4,0},{5,1},{6,2},{7,3},{8,4},{9,5},{1... | collective-permute-start | bytes 4616 | tf_op jit(solution)/shard_map/ppermute | solution.py:23
  169.0 5.1 %copy-start.20 = (f32[16,256]{1,0:T(8,128)S(1)}, f32[16,256]{1,0:T(8,128)}, u32[]{:S(2)}) copy-start(f32[16,256]{1,0:T(8,128)} %convert_bitcast_fusion) | copy-start | bytes 49156
  170.4 3.7 %collective-permute-start.25 = (f32[8,256]{1,0:T(8,128)S(1)}, f32[8,256]{1,0:T(8,128)S(1)}, u32[]{:S(2)}, u32[]{:S(2)}) collective-permute-start(f32[8,256]{1,0:T(8,128)S(1)} %copy.678), channel_id=1, source_target_pairs={{0,16},{16,0},{1,17},{17,1},{2,18},{18,2},{3,19},{19,3},{4,20},{20... | collective-permute-start | bytes 24584 | tf_op jit(solution)/shard_map/ppermute | solution.py:33
  174.1 99.5 %copy-start.21 = (f32[1,16,256]{2,1,0:T(8,128)}, f32[1,16,256]{2,1,0:T(8,128)S(1)}, u32[]{:S(2)}) copy-start(f32[1,16,256]{2,1,0:T(8,128)S(1)} %fusion.32) | copy-start | bytes 49156
  (5 other events, 4.3 us)
Sparse Core Ops, SparseCore 0:
  169.2 99.8 all-reduce.10
where the time goes:
time: 282 us; the launch traced here: 281 us
  waiting for transfers between devices  99.4 us (35%)
  local copies, waits for them, and re-layouts  78.2 us (28%)
  starting transfers between devices  43 us (15%)
  between operations  27.2 us (10%)
  other arithmetic  24.3 us (9%)
  matrix products  8.41 us (3%)
    psum x1, waiting for transfers between devices, body(): leading_gate_total = lax.psum(first_local, 'face')  94.9 us
    ppermute x24, starting transfers between devices, shifted(): return lax.ppermute(value, axis, pairs)  39.5 us
    scatter-add x27, local copies, waits for them, and re-layouts, fold(): prognosis_outcome = prognosis_outcome.at[:, vertical_place:vertical_place...  18.1 us
    eq x22, local copies, waits for them, and re-layouts, gate_keep(): keep = (low[..., None] == lanes) | (high[..., None] == lanes)  16.4 us
    add x21, other arithmetic, fold(): prognosis_outcome = prognosis_outcome.at[:, vertical_place:vertical_place...  11.2 us
    unnamed x90, local copies, waits for them, and re-layouts  8.82 us
    scatter x3, local copies, waits for them, and re-layouts, with_halo(): padded = padded.at[:, 0, 1:-1].set(south)  7.83 us
    another operation x5, other arithmetic  7.52 us
  transfers between devices with their start and end apart: 27, of which 4 were waited for; matrix products, arithmetic and copies ran while one was open for 25% of the time, Pallas kernels for 0%

commit v1 on v0

v1 whole, which is shorter than its diff:
```python
import functools

import jax
import jax.numpy as jnp
from jax import lax
from jax.experimental import pallas as pl
from jax.experimental.pallas import tpu as pltpu
from jax.sharding import PartitionSpec as P

FIELDS = 16
COUPLED = 8
ROW_TILES = 4
TS = 16
CELLS = TS * TS
STRIPS = 4 * TS
PADDED = 32
BF = jnp.bfloat16
F32 = jnp.float32

EDGE_MAP = (
    ((0, False), (2, True), (1, True), (3, False)),
    ((1, False), (3, True), (0, True), (2, False)),
    ((2, False), (1, False), (3, True), (0, True)),
    ((3, False), (0, False), (2, True), (1, True)),
)


def nn(x, y):
    return jnp.dot(x, y, preferred_element_type=F32)


def nt(x, y):
    return lax.dot_general(x, y, (((1,), (1,)), ((), ())), preferred_element_type=F32)


def tn(x, y):
    return lax.dot_general(x, y, (((0,), (0,)), ((), ())), preferred_element_type=F32)


def iota(shape, axis):
    return lax.broadcasted_iota(jnp.int32, shape, axis)


def split_low_high(gate, place):
    low = jnp.where(gate >= 5.0, 2.0, jnp.where(gate >= 3.0, 1.0, 0.0))
    high = jnp.where(gate == 0.0, 1.0, jnp.where((gate == 1.0) | (gate == 3.0), 2.0, 3.0))
    return jnp.where(low == place, 1.0, 0.0), jnp.where(high == place, 1.0, 0.0)


def silu_slope(v):
    sig = 1.0 / (1.0 + jnp.exp(-v))
    return v * sig, sig * (1.0 + v * (1.0 - sig))


def bit_order(count):
    bits = count.bit_length() - 1
    order = list(range(min(2, bits))) + list(range(bits - 1, 1, -1))
    pieces = []
    for slot in range(count):
        piece = 0
        for step, bit in enumerate(order):
            piece |= (slot >> (bits - 1 - step) & 1) << bit
        pieces.append(piece)
    return order, pieces


def kernel(
    count,
    turn,
    state,
    cot,
    sea,
    w1,
    w2_hbm,
    w3,
    gates1,
    gates2_hbm,
    gates3,
    up_out,
    adj_out,
    d1_out,
    d2_out,
    d3_out,
    w2,
    gates2,
    w2t,
    low2,
    high2,
    cols1,
    cols2,
    shift,
    acts,
    dh,
    w1m,
    w1pad,
    w1p,
    low1,
    high1,
    mask3,
    e0_send,
    e0_own,
    e0_partner,
    e0_inner,
    e1_send,
    e1_recv,
    h2_send,
    h2_recv,
    b2_send,
    b2_recv,
    b1_send,
    b1_recv,
    b0_send,
    b0_own,
    b0_partner,
    b0_inner_send,
    b0_inner,
    big,
    big_send,
    big_recv,
    small,
    small_send,
    small_recv,
    gathered,
    send_sem,
    recv_sem,
    load_sem,
):
    order, pieces = bit_order(count)
    steps = len(order)
    taps = w2.shape[0]
    rows = taps // count
    piece_rows = big.shape[1]
    comp = lax.axis_index("comp")
    me = lax.axis_index("face")
    other = 1 - comp
    used = [0]

    def copy_to(src, dst, component, face):
        index = used[0]
        used[0] += 1
        copy = pltpu.make_async_remote_copy(
            src_ref=src,
            dst_ref=dst,
            send_sem=send_sem.at[index],
            recv_sem=recv_sem.at[index],
            device_id=(component, face),
            device_id_type=pl.DeviceIdType.MESH,
        )
        copy.start()
        return copy

    def face_at(offset):
        return lax.rem(me + offset + count, count)

    forward = [face_at(1), face_at(-1), face_at(ROW_TILES), face_at(-ROW_TILES)]
    backward = [forward[1], forward[0], forward[3], forward[2]]
    mates = []
    for bit in order:
        mine = lax.rem(me // (1 << bit), 2)
        mates.append((mine, me + (1 - 2 * mine) * (1 << bit)))

    load_w2 = pltpu.make_async_copy(w2_hbm, w2, load_sem.at[0])
    load_g2 = pltpu.make_async_copy(gates2_hbm, gates2, load_sem.at[1])
    load_w2.start()
    load_g2.start()

    barrier = pltpu.get_barrier_semaphore()
    signals = 0
    targets = [(other, me)]
    targets += [(c, f) for c in (comp, other) for f in forward]
    targets += [(comp, mate) for _, mate in mates]
    for target in targets:
        pl.semaphore_signal(barrier, inc=1, device_id=target, device_id_type=pl.DeviceIdType.MESH)
        signals += 1

    strip = iota((STRIPS, 1), 0)
    side = strip // TS
    along = lax.rem(strip, TS)
    offsets = (1, -1, ROW_TILES, -ROW_TILES)
    edge_cell = jnp.zeros((STRIPS, 1), jnp.int32)
    for s in range(4):
        turns = turn[s, face_at(offsets[s])]
        for k in range(4):
            slot, flip = EDGE_MAP[s][k]
            j = TS - 1 - along if flip else along
            cell = (j * TS + TS - 1, j * TS, (TS - 1) * TS + j, j)[slot]
            edge_cell = jnp.where((side == s) & (turns == k), cell, edge_cell)
    pick = jnp.where(iota((STRIPS, CELLS), 1) == edge_cell, 1.0, 0.0).astype(BF)

    state_f = state[...].astype(F32)
    wide = jnp.concatenate([state_f, jnp.zeros((128 - FIELDS, CELLS), F32)], 0).astype(BF)
    e0_send[...] = nt(pick, wide).astype(BF)

    pl.semaphore_wait(barrier, signals)
    waits0 = [copy_to(state, e0_inner, other, me)]
    for component, landing in ((comp, e0_own), (other, e0_partner)):
        for s in range(4):
            part = pl.ds(s * TS, TS)
            waits0.append(copy_to(e0_send.at[part], landing.at[part], component, forward[s]))

    cell = iota((1, CELLS), 1)
    row, column = cell // TS, lax.rem(cell, TS)
    source = iota((CELLS + STRIPS, CELLS), 0)
    for a in range(3):
        for b in range(3):
            r, q = row + (a - 1), column + (b - 1)
            r_in, q_in = (r >= 0) & (r < TS), (q >= 0) & (q < TS)
            at = jnp.where(r_in & q_in, r * TS + q, -1)
            at = jnp.where(r_in & (q < 0), CELLS + r, at)
            at = jnp.where(r_in & (q >= TS), CELLS + TS + r, at)
            at = jnp.where(q_in & (r < 0), CELLS + 2 * TS + q, at)
            at = jnp.where(q_in & (r >= TS), CELLS + 3 * TS + q, at)
            shift[3 * a + b] = jnp.where(source == at, 1.0, 0.0).astype(BF)

    scale = jnp.where(comp == 1, sea[...].astype(F32), 1.0)
    cot_f = cot[...].astype(F32)
    g3 = (scale * cot_f).astype(BF)
    channel = iota((FIELDS, gates3.shape[1]), 0)
    gate3 = gates3[...].astype(F32)
    group = channel // 4
    gate_rows = jnp.where(
        group == 0,
        gate3[0:1],
        jnp.where(group == 1, gate3[1:2], jnp.where(group == 2, gate3[2:3], gate3[3:4])),
    )
    low3, high3 = split_low_high(gate_rows, lax.rem(channel, 4).astype(F32))
    keep3 = low3 + high3
    w3m = jnp.where(keep3 > 0.0, w3[...].astype(F32), 0.0).astype(BF)
    hidden = w1.shape[1]

    def tap(k):
        return slice(k * hidden, (k + 1) * hidden)

    strips_two = jnp.zeros((STRIPS, hidden), F32)
    for k in range(9):
        edge_grad = nt(shift[k, CELLS:, :], g3).astype(BF)
        strips_two += nn(edge_grad, w3m[:, tap(k)])
    b2_send[...] = strips_two.astype(BF)
    waits_b2 = []
    for s in range(4):
        part = pl.ds(s * TS, TS)
        waits_b2.append(copy_to(b2_send.at[part], b2_recv.at[part], comp, backward[s]))

    place = lax.rem(iota((1, hidden), 1), 4).astype(F32)
    spread = jnp.where(iota((hidden // 4, hidden), 0) == iota((hidden // 4, hidden), 1) // 4, 1.0, 0.0)
    spread = spread.astype(BF)
    rows_one = w1.shape[0]
    channels = rows_one // 9
    gate_one = tn(gates1[...].astype(F32).astype(BF), spread)
    lo, hi = split_low_high(gate_one, place)
    low1[...] = jnp.zeros_like(low1)
    high1[...] = jnp.zeros_like(high1)
    low1[pl.ds(0, rows_one)] = lo
    high1[pl.ds(0, rows_one)] = hi
    w1m[...] = jnp.where(lo + hi > 0.0, w1[...].astype(F32), 0.0)
    w1pad[...] = jnp.zeros_like(w1pad)
    for k in range(9):
        w1pad[pl.ds(k * PADDED, channels)] = w1m[pl.ds(k * channels, channels)]
    w1p[...] = w1pad[...].astype(BF)
    w1t = w1pad[...].T.astype(BF)

    load_w2.wait()
    load_g2.wait()
    if not rows % TS == 0:
        for ref in (low2, high2, cols1):
            ref[pl.ds(taps, 2 * TS)] = jnp.zeros((2 * TS, hidden), BF)
    for k in range(9):
        part = pl.ds(k * hidden, hidden)
        gate = tn(gates2[:, tap(k)].astype(F32).astype(BF), spread)
        lo, hi = split_low_high(gate, place)
        low2[part] = lo.astype(BF)
        high2[part] = hi.astype(BF)
        masked = jnp.where(lo + hi > 0.0, w2[part].astype(F32), 0.0)
        w2[part] = masked.astype(BF)
        w2t[:, tap(k)] = masked.T.astype(BF)

    def flipped(k):
        return shift[8 - k, :CELLS, :]

    for copy in waits0:
        copy.wait()
    inner = jnp.concatenate(
        [state_f, e0_inner[...].astype(F32)[:COUPLED], jnp.zeros((PADDED - FIELDS - COUPLED, CELLS), F32)], 0
    )
    own_t = e0_own[...].astype(F32).T
    partner_t = e0_partner[...].astype(F32).T
    halo = jnp.concatenate(
        [own_t[:FIELDS], partner_t[:COUPLED], jnp.zeros((PADDED - FIELDS - COUPLED, STRIPS), F32)], 0
    )
    field = jnp.concatenate([inner, halo], 1).astype(BF)
    cols0 = jnp.concatenate([nn(field, shift[k]) for k in range(9)], 0).astype(BF)
    act_one = nn(w1t, cols0)
    hid, slope_one = silu_slope(act_one)
    acts[...] = slope_one
    hid = hid.astype(BF)
    e1_send[...] = nt(pick, hid).astype(BF)
    waits1 = []
    for s in range(4):
        part = pl.ds(s * TS, TS)
        waits1.append(copy_to(e1_send.at[part], e1_recv.at[part], comp, forward[s]))

    for k in range(9):
        cols1[pl.ds(k * hidden, hidden)] = nn(hid, shift[k, :CELLS, :]).astype(BF)
    shifted3 = jnp.concatenate([nn(g3, flipped(k)) for k in range(9)], 0).astype(BF)
    stacked3 = jnp.concatenate([w3m[:, tap(k)] for k in range(9)], 0)
    dh[...] = tn(stacked3, shifted3)
    for copy in waits_b2:
        copy.wait()
    dh[...] += tn(b2_recv[...], pick)

    for copy in waits1:
        copy.wait()
    halo_t = e1_recv[...].astype(F32).T.astype(BF)
    for k in range(9):
        part = pl.ds(k * hidden, hidden)
        cols1[part] = cols1[part] + nn(halo_t, shift[k, CELLS:, :]).astype(BF)
    act_two = nn(w2t[...], cols1[pl.ds(0, taps)])
    hid, slope_two = silu_slope(act_two)
    g2 = (dh[...] * slope_two).astype(BF)
    hid = hid.astype(BF)

    strips_one = jnp.zeros((STRIPS, hidden), F32)
    for k in range(9):
        edge_grad = nt(shift[k, CELLS:, :], g2).astype(BF)
        strips_one += nt(edge_grad, w2[pl.ds(k * hidden, hidden)])
    b1_send[...] = strips_one.astype(BF)
    h2_send[...] = nt(pick, hid).astype(BF)
    waits_b1, waits_h2 = [], []
    for s in range(4):
        part = pl.ds(s * TS, TS)
        waits_b1.append(copy_to(b1_send.at[part], b1_recv.at[part], comp, backward[s]))
    for s in range(4):
        part = pl.ds(s * TS, TS)
        waits_h2.append(copy_to(h2_send.at[part], h2_recv.at[part], comp, forward[s]))

    lane, packed = iota((hidden, hidden // 2), 0) // 4, iota((hidden, hidden // 2), 1)
    pack_low = jnp.where(lane == packed, 1.0, 0.0).astype(BF)
    pack_high = jnp.where(lane + hidden // 4 == packed, 1.0, 0.0).astype(BF)

    def pack(term, low, high):
        return nn(term * low, pack_low) + nn(term * high, pack_high)

    def unpack(total, low, high):
        top = total.astype(BF)
        rest = (total - top.astype(F32)).astype(BF)
        return (nt(top, pack_low) + nt(rest, pack_low)) * low + (nt(top, pack_high) + nt(rest, pack_high)) * high

    aligned = rows % TS == 0
    slab = rows if aligned else piece_rows + TS

    def piece_part(index):
        return pl.ds(pl.multiple_of(index * rows // TS * TS, TS), slab)

    def settle(values, index):
        if aligned:
            return values
        return pltpu.roll(values, lax.rem(slab - lax.rem(index * rows, TS), slab), 0)[:piece_rows]

    def piece_term(index):
        part = piece_part(index)
        return settle(pack(nt(cols1[part], g2).astype(BF), low2[part], high2[part]), index)

    half = count // 2
    core = mates[0][0]
    for i in range(half):
        big_send[i] = piece_term(pieces[i] + (1 - core)).astype(BF)
    starts = [jnp.int32(0)]
    sent_at = [0]
    big_copies = [copy_to(big_send.at[pl.ds(0, half)], big_recv.at[pl.ds(0, half)], comp, mates[0][1])]
    for i in range(half):
        big[i] = piece_term(pieces[i] + core)

    total = jnp.zeros((hidden, CELLS), F32)
    for k in range(9):
        moved = nn(g2, flipped(k)).astype(BF)
        total += nn(w2[pl.ds(k * hidden, hidden)], moved)
    for copy in waits_b1:
        copy.wait()
    total += tn(b1_recv[...], pick)
    g1 = (total * acts[...]).astype(BF)

    back = nn(w1p[...], g1)
    back_zero = jnp.zeros((2 * PADDED, CELLS + STRIPS), F32)
    for k in range(9):
        piece = back[k * PADDED : (k + 1) * PADDED]
        top = piece.astype(BF)
        rest = (piece - top.astype(F32)).astype(BF)
        back_zero += nt(jnp.concatenate([top, rest], 0), shift[k])
    back_zero = back_zero[:PADDED] + back_zero[PADDED:]
    strips_zero = jnp.concatenate([back_zero[:, CELLS:], jnp.zeros((128 - PADDED, STRIPS), F32)], 0).T
    b0_send[...] = strips_zero.astype(BF)
    b0_inner_send[...] = back_zero[FIELDS : FIELDS + COUPLED, :CELLS]
    waits_b0 = [copy_to(b0_inner_send, b0_inner, other, me)]
    for component, landing in ((comp, b0_own), (other, b0_partner)):
        for s in range(4):
            part = pl.ds(s * TS, TS)
            waits_b0.append(copy_to(b0_send.at[part], landing.at[part], component, backward[s]))

    def fold_in(step, copy, held, landing):
        size = count >> (step + 1)
        offset = sum(count >> (s + 1) for s in range(step))
        copy.wait()
        for i in range(size):
            held[i] = held[i] + landing[offset + i].astype(F32)

    def pass_on(step, held, outgoing, landing):
        size = count >> (step + 1)
        offset = sum(count >> (s + 1) for s in range(step))
        mine, mate = mates[step]
        for i in range(size):
            gives = held[(1 - mine) * size + i]
            keeps = held[mine * size + i]
            outgoing[offset + i] = gives.astype(BF)
            held[i] = keeps
        return copy_to(
            outgoing.at[pl.ds(offset, size)], landing.at[pl.ds(offset, size)], comp, mate
        )

    big_copy = big_copies[0]
    fold_in(0, big_copy, big, big_recv)
    if steps > 1:
        big_copy = pass_on(1, big, big_send, big_recv)

    for copy in waits_h2:
        copy.wait()
    field = jnp.concatenate([hid, h2_recv[...].astype(F32).T.astype(BF)], 1)
    for k in range(9):
        cols2[pl.ds(k * hidden, hidden)] = nn(field, shift[k]).astype(BF)
    result = nn(w3m, cols2[...])
    up_out[...] = (state_f + scale * result).astype(BF)

    term_one = nt(cols0, g1)
    w1pad[...] = term_one
    w1m_rows = [w1pad[pl.ds(k * PADDED, channels)] for k in range(9)]
    w1m_rows.append(jnp.zeros((small.shape[0] * TS - rows_one, hidden), F32))
    term_one = jnp.concatenate(w1m_rows, 0).astype(BF)
    packed_one = pack(term_one, low1[...].astype(BF), high1[...].astype(BF))
    wide3 = small.shape[2] - hidden // 2
    for slot in range(count):
        index = pieces[slot]
        part3 = nt(g3, cols2[pl.ds(index * rows, rows)])
        mask3[index, :, pl.ds(0, rows)] = keep3[:, index * rows : (index + 1) * rows]
        small[slot, :, pl.ds(0, rows)] = part3
        small[slot, :, pl.ds(rows, wide3 - rows)] = jnp.zeros((FIELDS, wide3 - rows), F32)
        small[slot, :, pl.ds(wide3, hidden // 2)] = packed_one[index * TS : (index + 1) * TS]
    small_copy = pass_on(0, small, small_send, small_recv)

    for step in range(steps):
        if step > 0:
            fold_in(step, big_copy, big, big_recv)
            if step + 1 < steps:
                big_copy = pass_on(step + 1, big, big_send, big_recv)
        fold_in(step, small_copy, small, small_recv)
        if step + 1 < steps:
            small_copy = pass_on(step + 1, small, small_send, small_recv)

    my_slot = jnp.int32(0)
    for step in range(steps):
        my_slot = my_slot + mates[step][0] * (count >> (step + 1))
    gathered[my_slot] = small[0, :, pl.ds(wide3, hidden // 2)]
    d3_out[...] = small[0, :, pl.ds(0, rows)] * mask3[me, :, pl.ds(0, rows)]
    part = piece_part(me)
    low_mine, high_mine = (settle(ref[part].astype(F32), me) for ref in (low2, high2))
    d2_out[...] = unpack(big[0], low_mine, high_mine)
    start = my_slot
    for step in range(steps - 1, -1, -1):
        size = count >> (step + 1)
        mine, mate = mates[step]
        part = pl.ds(start, size)
        copy = copy_to(gathered.at[part], gathered.at[part], comp, mate)
        if step == steps - 1:
            for waiting in waits_b0:
                waiting.wait()
            returned = tn(b0_own[...], pick)
            coupled = tn(b0_partner[...], pick)
            own = cot_f + back_zero[:FIELDS, :CELLS] + returned[:FIELDS]
            top = own[:COUPLED] + b0_inner[...] + coupled[FIELDS : FIELDS + COUPLED]
            adj_out[...] = jnp.concatenate([top, own[COUPLED:]], 0)
        copy.wait()
        start = start - mine * size
    slot_of = [pieces.index(index) for index in range(count)]
    summed = jnp.concatenate([gathered[slot_of[i]] for i in range(-(-rows_one // TS))], 0)
    kept = summed.shape[0]
    whole = unpack(summed, low1[pl.ds(0, kept)], high1[pl.ds(0, kept)])
    d1_out[...] = whole[:rows_one]


def body(count, state, cotangent, land_sea, turn_table, w1, w2, w3, gates1, gates2, gates3):
    hidden = w1.shape[2]
    taps = w2.shape[1]
    rows = taps // count
    piece_rows = -(-rows // TS) * TS
    spare = taps if rows % TS == 0 else taps + 2 * TS
    wide3 = -(-rows // 128) * 128
    one_rows = max(count * TS, 256)
    vmem = pl.BlockSpec(memory_space=pltpu.VMEM)
    any_space = pl.BlockSpec(memory_space=pl.ANY)
    smem = pl.BlockSpec(memory_space=pltpu.SMEM)
    steps = count.bit_length() - 1
    copies = 9 + 4 + 4 + 4 + 4 + 9 + 3 * steps

    def half(*shape):
        return pltpu.VMEM(shape, BF)

    def full(*shape):
        return pltpu.VMEM(shape, F32)

    up, adj, d1, d2, d3 = pl.pallas_call(
        functools.partial(kernel, count),
        out_shape=(
            jax.ShapeDtypeStruct((FIELDS, CELLS), BF),
            jax.ShapeDtypeStruct((FIELDS, CELLS), F32),
            jax.ShapeDtypeStruct((w1.shape[1], hidden), F32),
            jax.ShapeDtypeStruct((piece_rows, hidden), F32),
            jax.ShapeDtypeStruct((FIELDS, rows), F32),
        ),
        in_specs=[smem, vmem, vmem, vmem, vmem, any_space, vmem, vmem, any_space, vmem],
        out_specs=(vmem,) * 5,
        scratch_shapes=[
            half(taps, hidden),
            pltpu.VMEM((hidden // 4, taps), jnp.int32),
            half(hidden, taps),
            half(spare, hidden),
            half(spare, hidden),
            half(spare, hidden),
            half(taps, hidden),
            half(9, CELLS + STRIPS, CELLS),
            full(hidden, CELLS),
            full(hidden, CELLS),
            full(w1.shape[1], hidden),
            full(9 * PADDED, hidden),
            half(9 * PADDED, hidden),
            full(one_rows, hidden),
            full(one_rows, hidden),
            full(count, FIELDS, wide3),
            half(STRIPS, 128),
            half(STRIPS, 128),
            half(STRIPS, 128),
            half(FIELDS, CELLS),
            half(STRIPS, hidden),
            half(STRIPS, hidden),
            half(STRIPS, hidden),
            half(STRIPS, hidden),
            half(STRIPS, hidden),
            half(STRIPS, hidden),
            half(STRIPS, hidden),
            half(STRIPS, hidden),
            half(STRIPS, 128),
            half(STRIPS, 128),
            half(STRIPS, 128),
            full(COUPLED, CELLS),
            full(COUPLED, CELLS),
            full(count // 2, piece_rows, hidden // 2),
            half(count, piece_rows, hidden // 2),
            half(count, piece_rows, hidden // 2),
            full(count, FIELDS, wide3 + hidden // 2),
            half(count, FIELDS, wide3 + hidden // 2),
            half(count, FIELDS, wide3 + hidden // 2),
            full(count, TS, hidden // 2),
            pltpu.SemaphoreType.DMA((copies,)),
            pltpu.SemaphoreType.DMA((copies,)),
            pltpu.SemaphoreType.DMA((2,)),
        ],
        compiler_params=pltpu.CompilerParams(
            collective_id=0, has_side_effects=True, vmem_limit_bytes=48 * 1024 * 1024
        ),
        cost_estimate=pl.CostEstimate(flops=2_000_000_000, bytes_accessed=4_000_000, transcendentals=200_000),
    )(
        turn_table.T,
        state[0],
        cotangent[0],
        land_sea.reshape(1, CELLS),
        w1[0],
        w2[0],
        w3[0].T,
        gates1[0].T,
        gates2[0].T,
        gates3[0].T,
    )
    return (up[None], adj[None], d1[None], d2[:rows].reshape(1, -1), d3.T.reshape(1, -1))


def solution(mesh):
    kernel_spec = P("comp", None, None)
    grid_spec = P("comp", None, "face")
    return jax.shard_map(
        functools.partial(body, mesh.shape["face"]),
        mesh=mesh,
        in_specs=(grid_spec, grid_spec, P("face"), P()) + (kernel_spec,) * 6,
        out_specs=(grid_spec, grid_spec, kernel_spec, P("comp", "face"), P("comp", "face")),
        check_vma=False,
    )
```

time: 282 us -> 59.6 us (0.21)
  waiting for transfers between devices: 99.4 us -> 0 us
  local copies, waits for them, and re-layouts: 78.2 us -> 12 us
  Pallas kernels: 0 us -> 46.4 us
  starting transfers between devices: 43 us -> 0 us
  between operations: 27.2 us -> 0.66 us
  other arithmetic: 24.3 us -> 0 us
  matrix products: 8.41 us -> 0 us
    psum x1 -> x0, waiting for transfers between devices: 94.9 us -> none  [body(): leading_gate_total = lax.psum(first_local, 'face')]
    pallas_call x0 -> x1, Pallas kernels: none -> 46.4 us  [body(): pl.pallas_call(functools.partial(kernel, count), out_shape=(jax.ShapeDtyp...]
    ppermute x26 -> x0, starting transfers between devices: 43 us -> none  [the longest x24 39.5 us: shifted(): return lax.ppermute(value, axis, pairs)]
    scatter-add x33 -> x0, local copies, waits for them, and re-layouts: 18.7 us -> none  [the longest x27 18.1 us: fold(): prognosis_outcome = prognosis_outcome.at[:, vertical_place:vertical_place...]
    scatter x12 -> x0, local copies, waits for them, and re-layouts: 16.8 us -> none  [the longest x3 7.83 us: with_halo(): padded = padded.at[:, 0, 1:-1].set(south)]
    eq x22 -> x0, local copies, waits for them, and re-layouts: 16.4 us -> none  [gate_keep(): keep = (low[..., None] == lanes) | (high[..., None] == lanes)]
    add x31 -> x0, other arithmetic: 12.3 us -> none  [the longest x21 11.2 us: fold(): prognosis_outcome = prognosis_outcome.at[:, vertical_place:vertical_place...]
    dot_general x9 -> x0, matrix products: 8.41 us -> none  [the longest x3 4.6 us: convolve_stencil(): lax.dot_general(kernel, columns, (((0,), (0,)), ((), ())), preferred_elem...]
  transfers between devices with their start and end apart: 27 -> 0, of which waited for: 4 -> 0; matrix products, arithmetic and copies ran while one was open for 25% -> 0% of each run, Pallas kernels for 0% -> 0%
where the time goes in v1:
time: 59.6 us; the launch traced here: 59.1 us
  Pallas kernels  46.4 us (78%)
  local copies, waits for them, and re-layouts  12 us (20%)
  between operations  0.66 us (1%)
    pallas_call x1, Pallas kernels, body(): pl.pallas_call(functools.partial(kernel, count), out_shape=(jax.ShapeDtyp...  46.4 us
    unnamed x24, local copies, waits for them, and re-layouts  11.2 us

profile of v1, /device:TPU:0, one launch (start us, length us, event | category | flops | bytes accessed | tf_op | source)
XLA Modules:
  0.0 59.1 jit_solution(366192423427933938)
XLA Ops:
  0.6 0.0 copy-start
  0.6 1.3 %copy-done = bf16[1,2304,256]{2,1,0:T(8,128)(2,1)S(1)} copy-done((bf16[1,2304,256]{2,1,0:T(8,128)(2,1)S(1)}, bf16[1,2304,256]{2,1,0:T(8,128)(2,1)}, u32[]{:S(2)}) %copy-start) | copy-done | bytes 1179672
  1.9 0.0 copy-start.1
  1.9 1.1 %copy-done.1 = s32[1,2304,64]{1,2,0:T(8,128)S(1)} copy-done((s32[1,2304,64]{1,2,0:T(8,128)S(1)}, s32[1,2304,64]{1,2,0:T(8,128)}, u32[]{:S(2)}) %copy-start.1) | copy-done | bytes 589848
  3.0 0.0 copy-start.2
  3.0 0.9 %copy-done.2 = bf16[1,216,256]{2,1,0:T(8,128)(2,1)S(1)} copy-done((bf16[1,216,256]{2,1,0:T(8,128)(2,1)S(1)}, bf16[1,216,256]{2,1,0:T(8,128)(2,1)}, u32[]{:S(2)}) %copy-start.2) | copy-done | bytes 110616
  3.9 0.0 copy-start.3
  3.9 0.9 %copy-done.3 = bf16[1,2304,16]{1,2,0:T(8,128)(2,1)S(1)} copy-done((bf16[1,2304,16]{1,2,0:T(8,128)(2,1)S(1)}, bf16[1,2304,16]{1,2,0:T(8,128)(2,1)}, u32[]{:S(2)}) %copy-start.3) | copy-done | bytes 73752
  4.8 0.0 copy-start.4
  4.8 0.8 %copy-done.4 = s32[1,216,64]{1,2,0:T(8,128)S(1)} copy-done((s32[1,216,64]{1,2,0:T(8,128)S(1)}, s32[1,216,64]{1,2,0:T(8,128)}, u32[]{:S(2)}) %copy-start.4) | copy-done | bytes 55320
  5.6 0.0 copy-start.5
  5.6 0.8 %copy-done.5 = s32[1,2304,4]{1,2,0:T(4,128)S(1)} copy-done((s32[1,2304,4]{1,2,0:T(4,128)S(1)}, s32[1,2304,4]{1,2,0:T(4,128)}, u32[]{:S(2)}) %copy-start.5) | copy-done | bytes 36888
  6.4 0.0 copy-start.6
  6.4 0.7 %copy-done.6 = bf16[1,16,256]{2,1,0:T(8,128)(2,1)S(1)} copy-done((bf16[1,16,256]{2,1,0:T(8,128)(2,1)S(1)}, bf16[1,16,256]{2,1,0:T(8,128)(2,1)}, u32[]{:S(2)}) %copy-start.6) | copy-done | bytes 8216
  7.1 0.0 copy-start.7
  7.1 0.7 %copy-done.7 = bf16[1,16,256]{2,1,0:T(8,128)(2,1)S(1)} copy-done((bf16[1,16,256]{2,1,0:T(8,128)(2,1)S(1)}, bf16[1,16,256]{2,1,0:T(8,128)(2,1)}, u32[]{:S(2)}) %copy-start.7) | copy-done | bytes 8216
  7.8 0.0 copy-start.8
  7.8 0.7 %copy-done.8 = s32[16,4]{0,1:T(4,128)S(1)} copy-done((s32[16,4]{0,1:T(4,128)S(1)}, s32[16,4]{0,1:T(4,128)}, u32[]{:S(2)}) %copy-start.8) | copy-done | bytes 280
  8.4 0.0 copy-start.9
  8.4 0.7 %copy-done.9 = s32[256]{0:T(256)S(1)} copy-done((s32[256]{0:T(256)S(1)}, s32[256]{0:T(256)}, u32[]{:S(2)}) %copy-start.9) | copy-done | bytes 1048
  9.1 46.4 %shard_map.137 = (bf16[16,256]{1,0:T(8,128)(2,1)S(1)}, f32[16,256]{1,0:T(8,128)S(1)}, f32[216,256]{1,0:T(8,128)S(1)}, f32[144,256]{1,0:T(8,128)S(1)}, f32[16,144]{1,0:T(8,128)S(1)}) custom-call(s32[4,16]{1,0:T(4,128)S(1)} %bitcast.38, bf16[16,256]{1,0:T(8,128)(2,1)S(1)} %bitcast.36, bf16[16,256]{1,0:T(8,128)(2,1)S(1)} %bitcast.37, s32[1,256]{1,0:T(1,128)S(1)} %bitcast.39, ...), custom_call_target="tpu_custom_call" | custom-call | flops 2000000000 | bytes 4000000 | tf_op jit(solution)/shard_map/pallas_call | solution.py:508
  55.6 0.1 copy.15
  55.7 0.7 %reshape.21 = f32[1,2304]{1,0:T(1,128)} reshape(f32[144,16]{1,0:T(8,128)S(1)} %copy.15) | data formatting | bytes 18432 | tf_op jit(solution)/shard_map/reshape | solution.py:580
  56.4 0.8 %copy.16 = f32[1,1,144,256]{3,1,2,0:T(1,128)} copy(f32[1,1,144,256]{3,2,1,0:T(8,128)S(1)} %bitcast.26) | data formatting | bytes 294912
  57.2 0.6 %copy.20 = bf16[1,16,256]{2,1,0:T(8,128)(2,1)} copy(bf16[1,16,256]{2,1,0:T(8,128)(2,1)S(1)} %bitcast.29) | data formatting | bytes 16384
  57.8 0.6 %copy.21 = f32[1,16,256]{2,1,0:T(8,128)} copy(f32[1,16,256]{2,1,0:T(8,128)S(1)} %bitcast.27) | data formatting | bytes 32768
  58.4 0.7 %copy.22 = f32[1,216,256]{2,1,0:T(8,128)} copy(f32[1,216,256]{2,1,0:T(8,128)S(1)} %bitcast.25) | data formatting | bytes 442368
Async XLA Ops:
  0.6 1.3 %copy-start = (bf16[1,2304,256]{2,1,0:T(8,128)(2,1)S(1)}, bf16[1,2304,256]{2,1,0:T(8,128)(2,1)}, u32[]{:S(2)}) copy-start(bf16[1,2304,256]{2,1,0:T(8,128)(2,1)} %param.15) | copy-start | bytes 3538948
  1.9 1.1 %copy-start.1 = (s32[1,2304,64]{1,2,0:T(8,128)S(1)}, s32[1,2304,64]{1,2,0:T(8,128)}, u32[]{:S(2)}) copy-start(s32[1,2304,64]{1,2,0:T(8,128)} %param.18) | copy-start | bytes 1769476
  3.0 0.9 %copy-start.2 = (bf16[1,216,256]{2,1,0:T(8,128)(2,1)S(1)}, bf16[1,216,256]{2,1,0:T(8,128)(2,1)}, u32[]{:S(2)}) copy-start(bf16[1,216,256]{2,1,0:T(8,128)(2,1)} %param.14) | copy-start | bytes 331780
  3.9 0.9 %copy-start.3 = (bf16[1,2304,16]{1,2,0:T(8,128)(2,1)S(1)}, bf16[1,2304,16]{1,2,0:T(8,128)(2,1)}, u32[]{:S(2)}) copy-start(bf16[1,2304,16]{1,2,0:T(8,128)(2,1)} %param.16) | copy-start | bytes 221188
  4.8 0.8 %copy-start.4 = (s32[1,216,64]{1,2,0:T(8,128)S(1)}, s32[1,216,64]{1,2,0:T(8,128)}, u32[]{:S(2)}) copy-start(s32[1,216,64]{1,2,0:T(8,128)} %param.17) | copy-start | bytes 165892
  5.6 0.8 %copy-start.5 = (s32[1,2304,4]{1,2,0:T(4,128)S(1)}, s32[1,2304,4]{1,2,0:T(4,128)}, u32[]{:S(2)}) copy-start(s32[1,2304,4]{1,2,0:T(4,128)} %param.19) | copy-start | bytes 110596
  6.4 0.7 %copy-start.6 = (bf16[1,16,256]{2,1,0:T(8,128)(2,1)S(1)}, bf16[1,16,256]{2,1,0:T(8,128)(2,1)}, u32[]{:S(2)}) copy-start(bf16[1,16,256]{2,1,0:T(8,128)(2,1)} %param.10) | copy-start | bytes 24580
  7.1 0.7 %copy-start.7 = (bf16[1,16,256]{2,1,0:T(8,128)(2,1)S(1)}, bf16[1,16,256]{2,1,0:T(8,128)(2,1)}, u32[]{:S(2)}) copy-start(bf16[1,16,256]{2,1,0:T(8,128)(2,1)} %param.11) | copy-start | bytes 24580
  7.8 0.7 %copy-start.8 = (s32[16,4]{0,1:T(4,128)S(1)}, s32[16,4]{0,1:T(4,128)}, u32[]{:S(2)}) copy-start(s32[16,4]{0,1:T(4,128)} %param.13) | copy-start | bytes 772
  8.4 0.7 %copy-start.9 = (s32[256]{0:T(256)S(1)}, s32[256]{0:T(256)}, u32[]{:S(2)}) copy-start(s32[256]{0:T(256)} %param.12) | copy-start | bytes 3076

commit v2 on v1

--- a/solution.py
+++ b/solution.py
@@ -52,37 +52,64 @@
     return v * sig, sig * (1.0 + v * (1.0 - sig))
 
 
-def bit_order(count):
-    bits = count.bit_length() - 1
-    order = list(range(min(2, bits))) + list(range(bits - 1, 1, -1))
+def slot_pieces(count, groups):
     pieces = []
     for slot in range(count):
-        piece = 0
-        for step, bit in enumerate(order):
-            piece |= (slot >> (bits - 1 - step) & 1) << bit
+        piece, below = 0, count
+        for low, size in groups:
+            below //= size
+            piece += (slot // below % size) << low
         pieces.append(piece)
-    return order, pieces
+    return pieces
+
+
+def stage_groups(count, first):
+    bits = count.bit_length() - 1
+    groups, low = [], 0
+    for width in first + [2] * bits:
+        width = min(width, bits - low)
+        if width > 0:
+            groups.append((low, 1 << width))
+            low += width
+    return groups
+
+
+def stage_offsets(count, groups):
+    held, start, places = count, 0, []
+    for _, size in groups:
+        held //= size
+        places.append((held, start))
+        start += held * (size - 1)
+    return places
 
 
 def kernel(
     count,
+    turn_hbm,
+    state_hbm,
+    cot_hbm,
+    sea_hbm,
+    w1_hbm,
+    w2_hbm,
+    w3_hbm,
+    gates1_hbm,
+    gates2_hbm,
+    gates3_hbm,
+    up_out,
+    adj_out,
+    d1_out,
+    d2_out,
+    d3_out,
     turn,
     state,
     cot,
     sea,
     w1,
-    w2_hbm,
+    w2,
     w3,
     gates1,
-    gates2_hbm,
+    gates2,
     gates3,
-    up_out,
-    adj_out,
-    d1_out,
-    d2_out,
-    d3_out,
-    w2,
-    gates2,
     w2t,
     low2,
     high2,
@@ -121,12 +148,13 @@
     small_send,
     small_recv,
     gathered,
+    turned,
     send_sem,
     recv_sem,
     load_sem,
 ):
-    order, pieces = bit_order(count)
-    steps = len(order)
+    big_groups, small_groups = stage_groups(count, [1, 1]), stage_groups(count, [2])
+    pieces, small_pieces = slot_pieces(count, big_groups), slot_pieces(count, small_groups)
     taps = w2.shape[0]
     rows = taps // count
     piece_rows = big.shape[1]
@@ -154,25 +182,63 @@
 
     forward = [face_at(1), face_at(-1), face_at(ROW_TILES), face_at(-ROW_TILES)]
     backward = [forward[1], forward[0], forward[3], forward[2]]
-    mates = []
-    for bit in order:
-        mine = lax.rem(me // (1 << bit), 2)
-        mates.append((mine, me + (1 - 2 * mine) * (1 << bit)))
-
-    load_w2 = pltpu.make_async_copy(w2_hbm, w2, load_sem.at[0])
-    load_g2 = pltpu.make_async_copy(gates2_hbm, gates2, load_sem.at[1])
-    load_w2.start()
-    load_g2.start()
+
+    def digit_of(group):
+        low, size = group
+        return lax.rem(me // (1 << low), size)
+
+    def mate_of(group, distance):
+        low, size = group
+        digit = digit_of(group)
+        target = lax.rem(digit + distance, size)
+        return target, me + (target - digit) * (1 << low)
+
 
     barrier = pltpu.get_barrier_semaphore()
     signals = 0
     targets = [(other, me)]
     targets += [(c, f) for c in (comp, other) for f in forward]
-    targets += [(comp, mate) for _, mate in mates]
+    for group in big_groups + small_groups:
+        targets += [(comp, mate_of(group, distance)[1]) for distance in range(1, group[1])]
     for target in targets:
         pl.semaphore_signal(barrier, inc=1, device_id=target, device_id_type=pl.DeviceIdType.MESH)
         signals += 1
 
+    loads = []
+    for index, (outside, inside) in enumerate(
+        (
+            (turn_hbm, turn),
+            (state_hbm, state),
+            (gates3_hbm, gates3),
+            (w3_hbm, w3),
+            (cot_hbm, cot),
+            (sea_hbm, sea),
+            (gates1_hbm, gates1),
+            (w1_hbm, w1),
+            (gates2_hbm, gates2),
+            (w2_hbm, w2),
+        )
+    ):
+        load = pltpu.make_async_copy(outside, inside, load_sem.at[index])
+        load.start()
+        loads.append(load)
+
+    cell = iota((1, CELLS), 1)
+    row, column = cell // TS, lax.rem(cell, TS)
+    source = iota((CELLS + STRIPS, CELLS), 0)
+    for a in range(3):
+        for b in range(3):
+            r, q = row + (a - 1), column + (b - 1)
+            r_in, q_in = (r >= 0) & (r < TS), (q >= 0) & (q < TS)
+            at = jnp.where(r_in & q_in, r * TS + q, -1)
+            at = jnp.where(r_in & (q < 0), CELLS + r, at)
+            at = jnp.where(r_in & (q >= TS), CELLS + TS + r, at)
+            at = jnp.where(q_in & (r < 0), CELLS + 2 * TS + q, at)
+            at = jnp.where(q_in & (r >= TS), CELLS + 3 * TS + q, at)
+            shift[3 * a + b] = jnp.where(source == at, 1.0, 0.0).astype(BF)
+
+    for load in loads[:2]:
+        load.wait()
     strip = iota((STRIPS, 1), 0)
     side = strip // TS
     along = lax.rem(strip, TS)
@@ -198,20 +264,8 @@
             part = pl.ds(s * TS, TS)
             waits0.append(copy_to(e0_send.at[part], landing.at[part], component, forward[s]))
 
-    cell = iota((1, CELLS), 1)
-    row, column = cell // TS, lax.rem(cell, TS)
-    source = iota((CELLS + STRIPS, CELLS), 0)
-    for a in range(3):
-        for b in range(3):
-            r, q = row + (a - 1), column + (b - 1)
-            r_in, q_in = (r >= 0) & (r < TS), (q >= 0) & (q < TS)
-            at = jnp.where(r_in & q_in, r * TS + q, -1)
-            at = jnp.where(r_in & (q < 0), CELLS + r, at)
-            at = jnp.where(r_in & (q >= TS), CELLS + TS + r, at)
-            at = jnp.where(q_in & (r < 0), CELLS + 2 * TS + q, at)
-            at = jnp.where(q_in & (r >= TS), CELLS + 3 * TS + q, at)
-            shift[3 * a + b] = jnp.where(source == at, 1.0, 0.0).astype(BF)
-
+    for load in loads[2:6]:
+        load.wait()
     scale = jnp.where(comp == 1, sea[...].astype(F32), 1.0)
     cot_f = cot[...].astype(F32)
     g3 = (scale * cot_f).astype(BF)
@@ -241,6 +295,8 @@
         part = pl.ds(s * TS, TS)
         waits_b2.append(copy_to(b2_send.at[part], b2_recv.at[part], comp, backward[s]))
 
+    for load in loads[6:8]:
+        load.wait()
     place = lax.rem(iota((1, hidden), 1), 4).astype(F32)
     spread = jnp.where(iota((hidden // 4, hidden), 0) == iota((hidden // 4, hidden), 1) // 4, 1.0, 0.0)
     spread = spread.astype(BF)
@@ -259,12 +315,12 @@
     w1p[...] = w1pad[...].astype(BF)
     w1t = w1pad[...].T.astype(BF)
 
-    load_w2.wait()
-    load_g2.wait()
+    for load in loads[8:]:
+        load.wait()
     if not rows % TS == 0:
         for ref in (low2, high2, cols1):
             ref[pl.ds(taps, 2 * TS)] = jnp.zeros((2 * TS, hidden), BF)
-    for k in range(9):
+    def mask_middle(k):
         part = pl.ds(k * hidden, hidden)
         gate = tn(gates2[:, tap(k)].astype(F32).astype(BF), spread)
         lo, hi = split_low_high(gate, place)
@@ -273,6 +329,9 @@
         masked = jnp.where(lo + hi > 0.0, w2[part].astype(F32), 0.0)
         w2[part] = masked.astype(BF)
         w2t[:, tap(k)] = masked.T.astype(BF)
+
+    for k in range(4):
+        mask_middle(k)
 
     def flipped(k):
         return shift[8 - k, :CELLS, :]
@@ -299,6 +358,8 @@
         part = pl.ds(s * TS, TS)
         waits1.append(copy_to(e1_send.at[part], e1_recv.at[part], comp, forward[s]))
 
+    for k in range(4, 9):
+        mask_middle(k)
     for k in range(9):
         cols1[pl.ds(k * hidden, hidden)] = nn(hid, shift[k, :CELLS, :]).astype(BF)
     shifted3 = jnp.concatenate([nn(g3, flipped(k)) for k in range(9)], 0).astype(BF)
@@ -356,24 +417,59 @@
             return values
         return pltpu.roll(values, lax.rem(slab - lax.rem(index * rows, TS), slab), 0)[:piece_rows]
 
-    def piece_term(index):
-        part = piece_part(index)
-        return settle(pack(nt(cols1[part], g2).astype(BF), low2[part], high2[part]), index)
+    def gather_rows(ref, indices):
+        return jnp.concatenate([ref[piece_part(index)] for index in indices], 0)
+
+    def piece_terms(indices):
+        term = nt(gather_rows(cols1, indices), g2).astype(BF)
+        packed = pack(term, gather_rows(low2, indices), gather_rows(high2, indices))
+        return [settle(packed[i * slab : (i + 1) * slab], index) for i, index in enumerate(indices)]
+
+    def start_stage(groups, stage, held, outgoing, landing):
+        size, start = stage_offsets(count, groups)[stage]
+        group = groups[stage]
+        copies = []
+        for distance in range(1, group[1]):
+            target, mate = mate_of(group, distance)
+            at = start + (distance - 1) * size
+            for i in range(size):
+                outgoing[at + i] = held[target * size + i].astype(BF)
+            part = pl.ds(at, size)
+            copies.append(copy_to(outgoing.at[part], landing.at[part], comp, mate))
+        return copies
+
+    def end_stage(groups, stage, held, landing, copies):
+        size, start = stage_offsets(count, groups)[stage]
+        mine = digit_of(groups[stage])
+        for copy in copies:
+            copy.wait()
+        for i in range(size):
+            total = held[mine * size + i]
+            for distance in range(1, groups[stage][1]):
+                total = total + landing[start + (distance - 1) * size + i].astype(F32)
+            held[i] = total
 
     half = count // 2
-    core = mates[0][0]
-    for i in range(half):
-        big_send[i] = piece_term(pieces[i] + (1 - core)).astype(BF)
-    starts = [jnp.int32(0)]
-    sent_at = [0]
-    big_copies = [copy_to(big_send.at[pl.ds(0, half)], big_recv.at[pl.ds(0, half)], comp, mates[0][1])]
-    for i in range(half):
-        big[i] = piece_term(pieces[i] + core)
+    core = digit_of(big_groups[0])
+    for i, packed in enumerate(piece_terms([pieces[i] + (1 - core) for i in range(half)])):
+        big_send[i] = packed.astype(BF)
+    first = pl.ds(0, half)
+    sibling = mate_of(big_groups[0], 1)[1]
+    big_copy = copy_to(big_send.at[first], big_recv.at[first], comp, sibling)
+    own_terms = piece_terms([pieces[i] + core for i in range(half)])
+    big_copy.wait()
+    for i, packed in enumerate(own_terms):
+        big[i] = packed + big_recv[i].astype(F32)
+    big_copies = []
+    if len(big_groups) > 1:
+        big_copies = start_stage(big_groups, 1, big, big_send, big_recv)
 
     total = jnp.zeros((hidden, CELLS), F32)
     for k in range(9):
         moved = nn(g2, flipped(k)).astype(BF)
         total += nn(w2[pl.ds(k * hidden, hidden)], moved)
+    for k in range(9):
+        cols2[pl.ds(k * hidden, hidden)] = nn(hid, shift[k, :CELLS, :]).astype(BF)
     for copy in waits_b1:
         copy.wait()
     total += tn(b1_recv[...], pick)
@@ -396,38 +492,12 @@
             part = pl.ds(s * TS, TS)
             waits_b0.append(copy_to(b0_send.at[part], landing.at[part], component, backward[s]))
 
-    def fold_in(step, copy, held, landing):
-        size = count >> (step + 1)
-        offset = sum(count >> (s + 1) for s in range(step))
-        copy.wait()
-        for i in range(size):
-            held[i] = held[i] + landing[offset + i].astype(F32)
-
-    def pass_on(step, held, outgoing, landing):
-        size = count >> (step + 1)
-        offset = sum(count >> (s + 1) for s in range(step))
-        mine, mate = mates[step]
-        for i in range(size):
-            gives = held[(1 - mine) * size + i]
-            keeps = held[mine * size + i]
-            outgoing[offset + i] = gives.astype(BF)
-            held[i] = keeps
-        return copy_to(
-            outgoing.at[pl.ds(offset, size)], landing.at[pl.ds(offset, size)], comp, mate
-        )
-
-    big_copy = big_copies[0]
-    fold_in(0, big_copy, big, big_recv)
-    if steps > 1:
-        big_copy = pass_on(1, big, big_send, big_recv)
-
     for copy in waits_h2:
         copy.wait()
-    field = jnp.concatenate([hid, h2_recv[...].astype(F32).T.astype(BF)], 1)
-    for k in range(9):
-        cols2[pl.ds(k * hidden, hidden)] = nn(field, shift[k]).astype(BF)
-    result = nn(w3m, cols2[...])
-    up_out[...] = (state_f + scale * result).astype(BF)
+    halo_t = h2_recv[...].astype(F32).T.astype(BF)
+    for k in range(9):
+        part = pl.ds(k * hidden, hidden)
+        cols2[part] = cols2[part] + nn(halo_t, shift[k, CELLS:, :]).astype(BF)
 
     term_one = nt(cols0, g1)
     w1pad[...] = term_one
@@ -437,38 +507,55 @@
     packed_one = pack(term_one, low1[...].astype(BF), high1[...].astype(BF))
     wide3 = small.shape[2] - hidden // 2
     for slot in range(count):
-        index = pieces[slot]
+        index = small_pieces[slot]
         part3 = nt(g3, cols2[pl.ds(index * rows, rows)])
         mask3[index, :, pl.ds(0, rows)] = keep3[:, index * rows : (index + 1) * rows]
         small[slot, :, pl.ds(0, rows)] = part3
         small[slot, :, pl.ds(rows, wide3 - rows)] = jnp.zeros((FIELDS, wide3 - rows), F32)
         small[slot, :, pl.ds(wide3, hidden // 2)] = packed_one[index * TS : (index + 1) * TS]
-    small_copy = pass_on(0, small, small_send, small_recv)
-
-    for step in range(steps):
-        if step > 0:
-            fold_in(step, big_copy, big, big_recv)
-            if step + 1 < steps:
-                big_copy = pass_on(step + 1, big, big_send, big_recv)
-        fold_in(step, small_copy, small, small_recv)
-        if step + 1 < steps:
-            small_copy = pass_on(step + 1, small, small_send, small_recv)
-
+    small_copies = start_stage(small_groups, 0, small, small_send, small_recv)
+    result = nn(w3m, cols2[...])
+    up_out[...] = (state_f + scale * result).astype(BF)
+
+    for stage in range(max(len(big_groups) - 1, len(small_groups))):
+        if stage + 1 < len(big_groups):
+            end_stage(big_groups, stage + 1, big, big_recv, big_copies)
+            if stage + 2 < len(big_groups):
+                big_copies = start_stage(big_groups, stage + 2, big, big_send, big_recv)
+        if stage < len(small_groups):
+            end_stage(small_groups, stage, small, small_recv, small_copies)
+            if stage + 1 < len(small_groups):
+                small_copies = start_stage(small_groups, stage + 1, small, small_send, small_recv)
+
+    places = stage_offsets(count, small_groups)
     my_slot = jnp.int32(0)
-    for step in range(steps):
-        my_slot = my_slot + mates[step][0] * (count >> (step + 1))
+    for group, (size, _) in zip(small_groups, places):
+        my_slot = my_slot + digit_of(group) * size
     gathered[my_slot] = small[0, :, pl.ds(wide3, hidden // 2)]
-    d3_out[...] = small[0, :, pl.ds(0, rows)] * mask3[me, :, pl.ds(0, rows)]
-    part = piece_part(me)
-    low_mine, high_mine = (settle(ref[part].astype(F32), me) for ref in (low2, high2))
-    d2_out[...] = unpack(big[0], low_mine, high_mine)
     start = my_slot
-    for step in range(steps - 1, -1, -1):
-        size = count >> (step + 1)
-        mine, mate = mates[step]
+    for stage in range(len(small_groups) - 1, -1, -1):
+        group, size = small_groups[stage], places[stage][0]
         part = pl.ds(start, size)
-        copy = copy_to(gathered.at[part], gathered.at[part], comp, mate)
-        if step == steps - 1:
+        copies = [
+            copy_to(gathered.at[part], gathered.at[part], comp, mate_of(group, distance)[1])
+            for distance in range(1, group[1])
+        ]
+        if stage == len(small_groups) - 1:
+            mine3 = small[0, :, pl.ds(0, rows)] * mask3[me, :, pl.ds(0, rows)]
+            if rows % 8 == 0:
+                turned[...] = jnp.concatenate([mine3, jnp.zeros((128 - FIELDS, rows), F32)], 0).T
+                lines = jnp.concatenate(
+                    [turned[pl.ds(u, rows // 8, stride=8), :][:, :FIELDS] for u in range(8)], 1
+                )
+                for j in range(rows // 8):
+                    d3_out[:, pl.ds(j * 128, 128)] = lines[j : j + 1]
+            else:
+                d3_out[...] = mine3
+            part = piece_part(me)
+            low_mine, high_mine = (settle(ref[part].astype(F32), me) for ref in (low2, high2))
+            mine2 = unpack(big[0], low_mine, high_mine)
+            for side in range(2):
+                d2_out[pl.ds(side, piece_rows, stride=2), :] = mine2[:, side * 128 : (side + 1) * 128]
             for waiting in waits_b0:
                 waiting.wait()
             returned = tn(b0_own[...], pick)
@@ -476,9 +563,10 @@
             own = cot_f + back_zero[:FIELDS, :CELLS] + returned[:FIELDS]
             top = own[:COUPLED] + b0_inner[...] + coupled[FIELDS : FIELDS + COUPLED]
             adj_out[...] = jnp.concatenate([top, own[COUPLED:]], 0)
-        copy.wait()
-        start = start - mine * size
-    slot_of = [pieces.index(index) for index in range(count)]
+        for copy in copies:
+            copy.wait()
+        start = start - digit_of(group) * size
+    slot_of = [small_pieces.index(index) for index in range(count)]
     summed = jnp.concatenate([gathered[slot_of[i]] for i in range(-(-rows_one // TS))], 0)
     kept = summed.shape[0]
     whole = unpack(summed, low1[pl.ds(0, kept)], high1[pl.ds(0, kept)])
@@ -495,9 +583,11 @@
     one_rows = max(count * TS, 256)
     vmem = pl.BlockSpec(memory_space=pltpu.VMEM)
     any_space = pl.BlockSpec(memory_space=pl.ANY)
-    smem = pl.BlockSpec(memory_space=pltpu.SMEM)
-    steps = count.bit_length() - 1
-    copies = 9 + 4 + 4 + 4 + 4 + 9 + 3 * steps
+    copies = 34
+    for groups, times in ((stage_groups(count, [1, 1]), 1), (stage_groups(count, [2]), 2)):
+        copies += times * sum(size - 1 for _, size in groups)
+    hbm = pl.BlockSpec(memory_space=pltpu.HBM)
+    shape3 = (1, rows * FIELDS) if rows % 8 == 0 else (FIELDS, rows)
 
     def half(*shape):
         return pltpu.VMEM(shape, BF)
@@ -511,14 +601,22 @@
             jax.ShapeDtypeStruct((FIELDS, CELLS), BF),
             jax.ShapeDtypeStruct((FIELDS, CELLS), F32),
             jax.ShapeDtypeStruct((w1.shape[1], hidden), F32),
-            jax.ShapeDtypeStruct((piece_rows, hidden), F32),
-            jax.ShapeDtypeStruct((FIELDS, rows), F32),
+            jax.ShapeDtypeStruct((2 * piece_rows, 128), F32),
+            jax.ShapeDtypeStruct(shape3, F32),
         ),
-        in_specs=[smem, vmem, vmem, vmem, vmem, any_space, vmem, vmem, any_space, vmem],
+        in_specs=[hbm] * 10,
         out_specs=(vmem,) * 5,
         scratch_shapes=[
+            pltpu.SMEM(turn_table.shape[::-1], jnp.int32),
+            half(FIELDS, CELLS),
+            half(FIELDS, CELLS),
+            pltpu.VMEM((1, CELLS), jnp.int32),
+            half(w1.shape[1], hidden),
             half(taps, hidden),
+            half(FIELDS, taps),
+            pltpu.VMEM((hidden // 4, w1.shape[1]), jnp.int32),
             pltpu.VMEM((hidden // 4, taps), jnp.int32),
+            pltpu.VMEM((FIELDS // 4, taps), jnp.int32),
             half(hidden, taps),
             half(spare, hidden),
             half(spare, hidden),
@@ -557,12 +655,13 @@
             half(count, FIELDS, wide3 + hidden // 2),
             half(count, FIELDS, wide3 + hidden // 2),
             full(count, TS, hidden // 2),
+            full(rows, 128),
             pltpu.SemaphoreType.DMA((copies,)),
             pltpu.SemaphoreType.DMA((copies,)),
-            pltpu.SemaphoreType.DMA((2,)),
+            pltpu.SemaphoreType.DMA((10,)),
         ],
         compiler_params=pltpu.CompilerParams(
-            collective_id=0, has_side_effects=True, vmem_limit_bytes=48 * 1024 * 1024
+            collective_id=0, has_side_effects=True, vmem_limit_bytes=64 * 1024 * 1024
         ),
         cost_estimate=pl.CostEstimate(flops=2_000_000_000, bytes_accessed=4_000_000, transcendentals=200_000),
     )(
@@ -577,7 +676,31 @@
         gates2[0].T,
         gates3[0].T,
     )
-    return (up[None], adj[None], d1[None], d2[:rows].reshape(1, -1), d3.T.reshape(1, -1))
+    results = (up, adj, d1, d2, d3)
+    lead = (1, 1, 1, 0, 0)
+
+    def write_all(*refs):
+        copies = []
+        for index in range(5):
+            target = refs[5 + index].at[0] if lead[index] else refs[5 + index]
+            copies.append(pltpu.make_async_copy(refs[index], target, refs[10].at[index]))
+            copies[-1].start()
+        for copy in copies:
+            copy.wait()
+
+    up, adj, d1, d2, d3 = pl.pallas_call(
+        write_all,
+        out_shape=tuple(
+            jax.ShapeDtypeStruct((1,) * extra + value.shape, value.dtype) for extra, value in zip(lead, results)
+        ),
+        in_specs=[any_space] * 5,
+        out_specs=(hbm,) * 5,
+        scratch_shapes=[pltpu.SemaphoreType.DMA((5,))],
+        compiler_params=pltpu.CompilerParams(vmem_limit_bytes=64 * 1024 * 1024),
+    )(*results)
+    if rows % 8:
+        d3 = d3.T
+    return (up, adj, d1, d2.reshape(1, -1)[:, : rows * hidden], d3.reshape(1, -1))
 
 
 def solution(mesh):

time: 59.6 us -> 53.7 us (0.901)
  local copies, waits for them, and re-layouts: 12 us -> 0 us
  Pallas kernels: 46.4 us -> 52.8 us
    pallas_call x0 -> x1, Pallas kernels: none -> 13.3 us  [body(): pl.pallas_call(write_all, out_shape=tuple((jax.ShapeDtypeStruct((1,) * ex...]
    unnamed x24 -> x0, local copies, waits for them, and re-layouts: 11.2 us -> none
    pallas_call x1, Pallas kernels: 46.4 us -> 39.5 us  [body(): pl.pallas_call(functools.partial(kernel, count), out_shape=(jax.ShapeDtyp...]
    reshape x1 -> x0, local copies, waits for them, and re-layouts: 0.7 us -> none  [body(): d3.T.reshape(1, -1)]
where the time goes in v2:
time: 53.7 us; the launch traced here: 53.5 us
  Pallas kernels  52.8 us (98%)
  between operations  0.64 us (1%)
    pallas_call x1, Pallas kernels, body(): pl.pallas_call(functools.partial(kernel, count), out_shape=(jax.ShapeDtyp...  39.5 us
    pallas_call x1, Pallas kernels, body(): pl.pallas_call(write_all, out_shape=tuple((jax.ShapeDtypeStruct((1,) * ex...  13.3 us

profile of v2, /device:TPU:0, one launch (start us, length us, event | category | flops | bytes accessed | tf_op | source)
XLA Modules:
  0.0 53.5 jit_solution(7713353143541546847)
XLA Ops:
  0.6 39.5 %shard_map.137 = (bf16[16,256]{1,0:T(8,128)(2,1)}, f32[16,256]{1,0:T(8,128)}, f32[216,256]{1,0:T(8,128)}, f32[288,128]{1,0:T(8,128)}, f32[1,2304]{1,0:T(1,128)}) custom-call(s32[4,16]{1,0:T(4,128)} %bitcast.28, bf16[16,256]{1,0:T(8,128)(2,1)} %bitcast.26, bf16[16,256]{1,0:T(8,128)(2,1)} %bitcast.27, s32[1,256]{1,0:T(1,128)} %bitcast.29, ...), custom_call_target="tpu_custom_call" | custom-call | flops 2000000000 | bytes 4000000 | tf_op jit(solution)/shard_map/pallas_call | solution.py:598
  40.1 13.3 %shard_map.138 = (bf16[1,16,256]{2,1,0:T(8,128)(2,1)}, f32[1,16,256]{2,1,0:T(8,128)}, f32[1,216,256]{2,1,0:T(8,128)}, f32[288,128]{1,0:T(8,128)}, f32[1,2304]{1,0:T(1,128)}) custom-call(bf16[16,256]{1,0:T(8,128)(2,1)} %get-tuple-element.15.refs_0_, f32[16,256]{1,0:T(8,128)} %get-tuple-element.16.refs_1_, f32[216,256]{1,0:T(8,128)} %get-tuple-element.17.refs_2_, ...), custom_call_target="tpu_custom_call" | custom-call | tf_op jit(solution)/shard_map/pallas_call | solution.py:691

commit v3 on v2

--- a/solution.py
+++ b/solution.py
@@ -144,9 +144,12 @@
     big,
     big_send,
     big_recv,
-    small,
-    small_send,
-    small_recv,
+    one,
+    one_send,
+    one_recv,
+    three,
+    three_send,
+    three_recv,
     gathered,
     turned,
     send_sem,
@@ -468,12 +471,22 @@
     for k in range(9):
         moved = nn(g2, flipped(k)).astype(BF)
         total += nn(w2[pl.ds(k * hidden, hidden)], moved)
-    for k in range(9):
-        cols2[pl.ds(k * hidden, hidden)] = nn(hid, shift[k, :CELLS, :]).astype(BF)
     for copy in waits_b1:
         copy.wait()
     total += tn(b1_recv[...], pick)
     g1 = (total * acts[...]).astype(BF)
+
+    one_rows = low1.shape[0]
+    term_one = nt(cols0, g1)
+    w1pad[...] = term_one
+    w1m_rows = [w1pad[pl.ds(k * PADDED, channels)] for k in range(9)]
+    w1m_rows.append(jnp.zeros((one_rows - rows_one, hidden), F32))
+    term_one = jnp.concatenate(w1m_rows, 0).astype(BF)
+    packed_one = pack(term_one, low1[...].astype(BF), high1[...].astype(BF))
+    for slot in range(count):
+        index = small_pieces[slot]
+        one[slot] = packed_one[index * TS : (index + 1) * TS]
+    one_copies = start_stage(small_groups, 0, one, one_send, one_recv)
 
     back = nn(w1p[...], g1)
     back_zero = jnp.zeros((2 * PADDED, CELLS + STRIPS), F32)
@@ -492,6 +505,13 @@
             part = pl.ds(s * TS, TS)
             waits_b0.append(copy_to(b0_send.at[part], landing.at[part], component, backward[s]))
 
+    if len(big_groups) > 1:
+        end_stage(big_groups, 1, big, big_recv, big_copies)
+        if len(big_groups) > 2:
+            big_copies = start_stage(big_groups, 2, big, big_send, big_recv)
+
+    for k in range(9):
+        cols2[pl.ds(k * hidden, hidden)] = nn(hid, shift[k, :CELLS, :]).astype(BF)
     for copy in waits_h2:
         copy.wait()
     halo_t = h2_recv[...].astype(F32).T.astype(BF)
@@ -499,39 +519,29 @@
         part = pl.ds(k * hidden, hidden)
         cols2[part] = cols2[part] + nn(halo_t, shift[k, CELLS:, :]).astype(BF)
 
-    term_one = nt(cols0, g1)
-    w1pad[...] = term_one
-    w1m_rows = [w1pad[pl.ds(k * PADDED, channels)] for k in range(9)]
-    w1m_rows.append(jnp.zeros((small.shape[0] * TS - rows_one, hidden), F32))
-    term_one = jnp.concatenate(w1m_rows, 0).astype(BF)
-    packed_one = pack(term_one, low1[...].astype(BF), high1[...].astype(BF))
-    wide3 = small.shape[2] - hidden // 2
+    end_stage(small_groups, 0, one, one_recv, one_copies)
+    if len(small_groups) > 1:
+        one_copies = start_stage(small_groups, 1, one, one_send, one_recv)
+
+    wide3 = three.shape[2]
     for slot in range(count):
         index = small_pieces[slot]
-        part3 = nt(g3, cols2[pl.ds(index * rows, rows)])
         mask3[index, :, pl.ds(0, rows)] = keep3[:, index * rows : (index + 1) * rows]
-        small[slot, :, pl.ds(0, rows)] = part3
-        small[slot, :, pl.ds(rows, wide3 - rows)] = jnp.zeros((FIELDS, wide3 - rows), F32)
-        small[slot, :, pl.ds(wide3, hidden // 2)] = packed_one[index * TS : (index + 1) * TS]
-    small_copies = start_stage(small_groups, 0, small, small_send, small_recv)
-    result = nn(w3m, cols2[...])
-    up_out[...] = (state_f + scale * result).astype(BF)
-
-    for stage in range(max(len(big_groups) - 1, len(small_groups))):
-        if stage + 1 < len(big_groups):
-            end_stage(big_groups, stage + 1, big, big_recv, big_copies)
-            if stage + 2 < len(big_groups):
-                big_copies = start_stage(big_groups, stage + 2, big, big_send, big_recv)
-        if stage < len(small_groups):
-            end_stage(small_groups, stage, small, small_recv, small_copies)
-            if stage + 1 < len(small_groups):
-                small_copies = start_stage(small_groups, stage + 1, small, small_send, small_recv)
+        three[slot, :, pl.ds(0, rows)] = nt(g3, cols2[pl.ds(index * rows, rows)])
+        if wide3 > rows:
+            three[slot, :, pl.ds(rows, wide3 - rows)] = jnp.zeros((FIELDS, wide3 - rows), F32)
+    three_copies = start_stage(small_groups, 0, three, three_send, three_recv)
+
+    for stage in range(1, len(small_groups)):
+        end_stage(small_groups, stage, one, one_recv, one_copies)
+        if stage + 1 < len(small_groups):
+            one_copies = start_stage(small_groups, stage + 1, one, one_send, one_recv)
 
     places = stage_offsets(count, small_groups)
     my_slot = jnp.int32(0)
     for group, (size, _) in zip(small_groups, places):
         my_slot = my_slot + digit_of(group) * size
-    gathered[my_slot] = small[0, :, pl.ds(wide3, hidden // 2)]
+    gathered[my_slot] = one[0]
     start = my_slot
     for stage in range(len(small_groups) - 1, -1, -1):
         group, size = small_groups[stage], places[stage][0]
@@ -541,7 +551,21 @@
             for distance in range(1, group[1])
         ]
         if stage == len(small_groups) - 1:
-            mine3 = small[0, :, pl.ds(0, rows)] * mask3[me, :, pl.ds(0, rows)]
+            result = nn(w3m, cols2[...])
+            up_out[...] = (state_f + scale * result).astype(BF)
+            end_stage(small_groups, 0, three, three_recv, three_copies)
+            if len(small_groups) > 1:
+                three_copies = start_stage(small_groups, 1, three, three_send, three_recv)
+        if stage == 0:
+            for step in range(1, len(small_groups)):
+                end_stage(small_groups, step, three, three_recv, three_copies)
+                if step + 1 < len(small_groups):
+                    three_copies = start_stage(small_groups, step + 1, three, three_send, three_recv)
+            for step in range(2, len(big_groups)):
+                end_stage(big_groups, step, big, big_recv, big_copies)
+                if step + 1 < len(big_groups):
+                    big_copies = start_stage(big_groups, step + 1, big, big_send, big_recv)
+            mine3 = three[0, :, pl.ds(0, rows)] * mask3[me, :, pl.ds(0, rows)]
             if rows % 8 == 0:
                 turned[...] = jnp.concatenate([mine3, jnp.zeros((128 - FIELDS, rows), F32)], 0).T
                 lines = jnp.concatenate(
@@ -584,7 +608,7 @@
     vmem = pl.BlockSpec(memory_space=pltpu.VMEM)
     any_space = pl.BlockSpec(memory_space=pl.ANY)
     copies = 34
-    for groups, times in ((stage_groups(count, [1, 1]), 1), (stage_groups(count, [2]), 2)):
+    for groups, times in ((stage_groups(count, [1, 1]), 1), (stage_groups(count, [2]), 3)):
         copies += times * sum(size - 1 for _, size in groups)
     hbm = pl.BlockSpec(memory_space=pltpu.HBM)
     shape3 = (1, rows * FIELDS) if rows % 8 == 0 else (FIELDS, rows)
@@ -651,9 +675,12 @@
             full(count // 2, piece_rows, hidden // 2),
             half(count, piece_rows, hidden // 2),
             half(count, piece_rows, hidden // 2),
-            full(count, FIELDS, wide3 + hidden // 2),
-            half(count, FIELDS, wide3 + hidden // 2),
-            half(count, FIELDS, wide3 + hidden // 2),
+            full(count, TS, hidden // 2),
+            half(count, TS, hidden // 2),
+            half(count, TS, hidden // 2),
+            full(count, FIELDS, wide3),
+            half(count, FIELDS, wide3),
+            half(count, FIELDS, wide3),
             full(count, TS, hidden // 2),
             full(rows, 128),
             pltpu.SemaphoreType.DMA((copies,)),
@@ -680,12 +707,16 @@
     lead = (1, 1, 1, 0, 0)
 
     def write_all(*refs):
-        copies = []
+        reads, writes = [], []
         for index in range(5):
+            reads.append(pltpu.make_async_copy(refs[index], refs[10 + index], refs[15].at[index]))
+            reads[-1].start()
+        for index in range(5):
+            reads[index].wait()
             target = refs[5 + index].at[0] if lead[index] else refs[5 + index]
-            copies.append(pltpu.make_async_copy(refs[index], target, refs[10].at[index]))
-            copies[-1].start()
-        for copy in copies:
+            writes.append(pltpu.make_async_copy(refs[10 + index], target, refs[15].at[5 + index]))
+            writes[-1].start()
+        for copy in writes:
             copy.wait()
 
     up, adj, d1, d2, d3 = pl.pallas_call(
@@ -695,7 +726,8 @@
         ),
         in_specs=[any_space] * 5,
         out_specs=(hbm,) * 5,
-        scratch_shapes=[pltpu.SemaphoreType.DMA((5,))],
+        scratch_shapes=[pltpu.VMEM(value.shape, value.dtype) for value in results]
+        + [pltpu.SemaphoreType.DMA((10,))],
         compiler_params=pltpu.CompilerParams(vmem_limit_bytes=64 * 1024 * 1024),
     )(*results)
     if rows % 8:

time: 53.7 us -> 42.2 us (0.79)
  Pallas kernels: 52.8 us -> 41.3 us
    pallas_call x1, Pallas kernels: 13.3 us -> 1.8 us  [body(): pl.pallas_call(write_all, out_shape=tuple((jax.ShapeDtypeStruct((1,) * ex...]
where the time goes in v3:
time: 42.2 us; the launch traced here: 42 us
  Pallas kernels  41.3 us (98%)
  between operations  0.64 us (2%)
    pallas_call x1, Pallas kernels, body(): pl.pallas_call(functools.partial(kernel, count), out_shape=(jax.ShapeDtyp...  39.5 us
    pallas_call x1, Pallas kernels, body(): pl.pallas_call(write_all, out_shape=tuple((jax.ShapeDtypeStruct((1,) * ex...  1.8 us

profile of v3, /device:TPU:0, one launch (start us, length us, event | category | flops | bytes accessed | tf_op | source)
XLA Modules:
  0.0 42.0 jit_solution(17271606726767816242)
XLA Ops:
  0.6 39.5 %shard_map.137 = (bf16[16,256]{1,0:T(8,128)(2,1)}, f32[16,256]{1,0:T(8,128)}, f32[216,256]{1,0:T(8,128)}, f32[288,128]{1,0:T(8,128)}, f32[1,2304]{1,0:T(1,128)}) custom-call(s32[4,16]{1,0:T(4,128)} %bitcast.28, bf16[16,256]{1,0:T(8,128)(2,1)} %bitcast.26, bf16[16,256]{1,0:T(8,128)(2,1)} %bitcast.27, s32[1,256]{1,0:T(1,128)} %bitcast.29, ...), custom_call_target="tpu_custom_call" | custom-call | flops 2000000000 | bytes 4000000 | tf_op jit(solution)/shard_map/pallas_call | solution.py:622
  40.2 1.8 %shard_map.138 = (bf16[1,16,256]{2,1,0:T(8,128)(2,1)}, f32[1,16,256]{2,1,0:T(8,128)}, f32[1,216,256]{2,1,0:T(8,128)}, f32[288,128]{1,0:T(8,128)}, f32[1,2304]{1,0:T(1,128)}) custom-call(bf16[16,256]{1,0:T(8,128)(2,1)} %get-tuple-element.15.refs_0_, f32[16,256]{1,0:T(8,128)} %get-tuple-element.16.refs_1_, f32[216,256]{1,0:T(8,128)} %get-tuple-element.17.refs_2_, ...), custom_call_target="tpu_custom_call" | custom-call | tf_op jit(solution)/shard_map/pallas_call | solution.py:722
